TPU v7x, 32 devices: a whole 2x2x4 slice. The times are simulated.
32 devices in a mesh: grp: 4 (over x, core), exc: 2 (over y), col: 4 (over z).
Axes of the slice: x: 2, y: 2, z: 4, core: 2. Of those that a mesh axis runs over, the one named last changes fastest.
Arguments:
- window_factor: float32 [1024, 8, 512], P('exc', 'grp'), may hold values from -0.375 to 0.375
- fitted_factor: float32 [1024, 512, 512], P('exc', 'col'), may hold values from -0.375 to 0.375
- pair_amps: float32 [16, 512, 512], P(None, 'col'), may hold values from -0.1875 to 0.1875
- cycle_amps: float32 [16, 32768], P(None, ('grp', 'exc')), may hold values from -6 to 6
- panel: float32 [32768, 4096], P(('grp', 'exc'), 'col'), may hold values from -0.03125 to 0.03125
Outputs:
- sigma: float32 [16, 4096], P(('grp', 'exc'), 'col')
All inputs are finite; a program needn't handle non-finite values.
Results may differ from a plain program's by a relative error of at most 0.0001.
Values sent between devices are 32-bit elements; how exact they have to be, the bound alone decides.
No kernel may reach another device: no remote copies, remote signals or barrier semaphores. Data moves between devices by JAX's collectives and lax.ppermute only.
A program may use at most 256 MiB of HBM per device.

v0:
```python
import jax
import jax.numpy as jnp
from jax import lax
from jax.sharding import PartitionSpec as P

NI = 2
NJ = 8


def shards(window_factor, fitted_factor, pair_amps, cycle_amps, panel):
    precise = lax.Precision.HIGHEST
    aux_count, virt_count, virtuals = window_factor.shape
    fit_count = fitted_factor.shape[1]
    amplitude = pair_amps.reshape(NI, NJ, fit_count, virtuals)
    inner = jnp.einsum("pac,ijdc->aijpd", window_factor, amplitude, precision=precise)
    inner_rows = inner.reshape(virt_count * NI * NJ, aux_count * fit_count)
    fitted_rows = fitted_factor.reshape(aux_count * fit_count, virtuals)
    ladder_terms = jnp.dot(
        inner_rows, fitted_rows, precision=precise, preferred_element_type=jnp.float32
    )
    ladder_terms = ladder_terms.reshape(virt_count * NI, NJ * virtuals)
    cycle_part = jnp.dot(cycle_amps, panel, precision=precise, preferred_element_type=jnp.float32)
    partial_value = lax.psum_scatter(ladder_terms, "col", scatter_dimension=1, tiled=True)
    ladder = lax.psum_scatter(partial_value, "exc", scatter_dimension=0, tiled=True)
    cycle = lax.psum_scatter(cycle_part, ("grp", "exc"), scatter_dimension=0, tiled=True)
    merged = ladder + cycle
    return merged


def solution(mesh):
    placed = (
        P("exc", "grp", None),
        P("exc", "col", None),
        P(None, "col", None),
        P(None, ("grp", "exc")),
        P(("grp", "exc"), "col"),
    )
    return jax.shard_map(
        shards, mesh=mesh, in_specs=placed, out_specs=P(("grp", "exc"), "col"), check_vma=False
    )
```

profile of v0, /device:TPU:0, one launch (start us, length us, event | category | flops | bytes accessed | tf_op | source)
XLA Modules:
  0.0 197.5 jit_solution(3870529988567956249)
XLA Ops:
  7.4 0.0 copy-start
  7.4 0.0 reduce-scatter.4.cloned.1.call-start
  7.4 1.6 copy-done
  9.0 17.6 %convolution_bitcast_fusion = f32[2,2,8,512,128]{3,4,0,2,1:T(8,128)} fusion(f32[2,8,128,512,1]{3,2,4,1,0:T(8,128)} %bitcast.24, f32[512,2,512,1,1]{2,1,0,4,3:T(2,128)S(1)} %bitcast.22), kind=kOutput, calls=%fused_computation.3 | convolution fusion | flops 12884901888 | bytes 14680064 | tf_op jit(solution)/shard_map/pac,ijdc->aijpd/dot_general | solution.py:15
  26.5 8.7 %copy.10 = f32[2,2,8,512,128]{4,3,2,1,0:T(8,128)} copy(f32[2,2,8,512,128]{3,4,0,2,1:T(8,128)} %convolution_bitcast_fusion) | data formatting | bytes 16777216 | tf_op jit(solution)/shard_map/pac,ijdc->aijpd/transpose | solution.py:15
  35.2 0.0 copy-start.1
  35.2 84.2 %fusion = f32[32,512]{1,0:T(8,128)S(1)} fusion(f32[65536,512]{1,0:T(8,128)} %bitcast.5, f32[4,8,512,128]{3,2,1,0:T(8,128)} %bitcast.23), kind=kOutput, calls=%fused_computation | convolution fusion | flops 12884901888 | bytes 142671872 | tf_op jit(solution)/shard_map/dot_general | solution.py:18
  119.5 2.0 %copy.15 = f32[4,4096]{0,1:T(8,128)} copy(f32[4,4096]{1,0:T(4,128)S(1)} %reshape.15) | data formatting | bytes 131072
  121.5 0.0 reduce-scatter.4.cloned.1.call-update
  121.5 0.0 copy-start.3
  121.5 0.0 copy-start.2
  121.5 0.0 all-reduce.4.cloned.1.call-start
  121.6 0.0 copy-done.1
  121.6 12.1 %fusion.4 = f32[16,1024]{1,0:T(8,128)} fusion(f32[16,4096]{1,0:T(8,128)S(1)} %copy-done.1, f32[4096,1024]{1,0:T(8,128)} %param.9), kind=kOutput, calls=%fused_computation.6 | convolution fusion | flops 805306368 | bytes 17104896 | tf_op jit(solution)/shard_map/dot_general | solution.py:22
  133.7 0.0 all-reduce.4.cloned.1.call-update
  133.7 0.0 copy-done.3
  133.8 0.7 dynamic-slice
  134.4 0.0 copy-done.2
  134.4 0.6 dynamic-slice.2
  136.3 31.9 %reduce-scatter.4.cloned.1.call-done = f32[1024,4]{1,0:T(8,128)} async-done(((f32[4096,4]{1,0:T(8,128)}), f32[1024,4]{1,0:T(8,128)}) %reduce-scatter.4.cloned.1.call-update) | async-done | bytes 16400
  168.2 1.2 copy.16
  169.5 8.2 %all-reduce = f32[4,1024]{1,0:T(4,128)S(1)} all-reduce(f32[4,1024]{1,0:T(4,128)S(1)} %copy.16), channel_id=3, replica_groups=mesh['grp'=4,'exc'=2,'col'=4] {'exc'}, use_global_device_ids=true, to_apply=%region_1.0.clone | all-reduce | flops 4096 | bytes 32768
  177.7 11.0 %all-reduce.4.cloned.1.call-done = f32[16,1024]{1,0:T(8,128)} async-done(((f32[16,1024]{1,0:T(8,128)}), f32[16,1024]{1,0:T(8,128)}) %all-reduce.4.cloned.1.call-update) | async-done | bytes 65552
  188.7 1.4 dynamic-slice_add_fusion
  (1 shorter events, 0.0 us)
Async XLA Ops:
  7.4 1.6 copy-start
  7.4 160.9 %reduce-scatter.4.cloned.1.call-start = ((), (), s32[]{:S(2)}) async-start(), calls=%async_computation.1 | async-start | bytes 2621440
  35.2 86.4 %copy-start.1 = (f32[16,4096]{1,0:T(8,128)S(1)}, f32[16,4096]{1,0:T(8,128)}, u32[]{:S(2)}) copy-start(f32[16,4096]{1,0:T(8,128)} %param.8) | copy-start | bytes 786436
  121.5 12.2 %copy-start.3 = (u32[32]{0:T(128)S(1)}, u32[32]{0:T(128)}, u32[]{:S(2)}) copy-start(u32[32]{0:T(128)} %constant.3) | copy-start | bytes 388
  121.5 12.9 %copy-start.2 = (u32[32]{0:T(128)S(1)}, u32[32]{0:T(128)}, u32[]{:S(2)}) copy-start(u32[32]{0:T(128)} %constant.7) | copy-start | bytes 388
  121.5 67.1 %all-reduce.4.cloned.1.call-start = ((), (), s32[]{:S(2)}) async-start(), calls=%async_computation.2 | async-start | bytes 131072
Sparse Core Ops, SparseCore 0:
  121.6 46.5 reduce-scatter.3
Sparse Core Ops, SparseCore 1:
  133.8 54.8 all-reduce.3
where the time goes:
time: 198 us; the launch traced here: 197 us
  matrix products  114 us (58%)
  waiting for transfers between devices  42.9 us (22%)
  between operations  16.2 us (8%)
  local copies, waits for them, and re-layouts  14.8 us (7%)
  blocking collectives  8.23 us (4%)
    dot_general x1, matrix products, shards(): jnp.dot(inner_rows, fitted_rows, precision=precise, preferred_element_typ...  84.2 us
    unnamed x4, waiting for transfers between devices  42.9 us
    dot_general x1, matrix products, shards(): jnp.einsum('pac,ijdc->aijpd', window_factor, amplitude, precision=precise)  17.6 us
    dot_general x1, matrix products, shards(): jnp.dot(cycle_amps, panel, precision=precise, preferred_element_type=jnp....  12.1 us
    transpose x1, local copies, waits for them, and re-layouts, shards(): jnp.einsum('pac,ijdc->aijpd', window_factor, amplitude, precision=precise)  8.69 us
    unnamed x1, blocking collectives  8.23 us
    unnamed x12, local copies, waits for them, and re-layouts  6.07 us
  transfers between devices with their start and end apart: 2, of which 2 were waited for; matrix products, arithmetic and copies ran while one was open for 7% of the time, Pallas kernels for 0%

commit v1 on v0

v1 whole, which is shorter than its diff:
```python
import functools

import jax
import jax.numpy as jnp
from jax import lax
from jax.experimental import pallas as pl
from jax.experimental.pallas import tpu as pltpu
from jax.sharding import PartitionSpec as P

NI = 2
NJ = 8
VMEM_BYTES = 56 * 1024 * 1024
LANES = 128


def split(x):
    high = x.astype(jnp.bfloat16)
    low = (x - high.astype(jnp.float32)).astype(jnp.bfloat16)
    return high, low


def dot(x, y):
    return jnp.dot(x, y, preferred_element_type=jnp.float32)


def dot_t(x, y):
    return lax.dot_general(x, y, (((1,), (1,)), ((), ())), preferred_element_type=jnp.float32)


def plain(window_factor, fitted_factor, pair_amps, cycle_amps, panel):
    precise = lax.Precision.HIGHEST
    aux_count, virt_count, virtuals = window_factor.shape
    fit_count = fitted_factor.shape[1]
    amplitude = pair_amps.reshape(NI, NJ, fit_count, virtuals)
    inner = jnp.einsum("pac,ijdc->aijpd", window_factor, amplitude, precision=precise)
    inner_rows = inner.reshape(virt_count * NI * NJ, aux_count * fit_count)
    fitted_rows = fitted_factor.reshape(aux_count * fit_count, virtuals)
    ladder_terms = jnp.dot(inner_rows, fitted_rows, precision=precise, preferred_element_type=jnp.float32)
    ladder_terms = ladder_terms.reshape(virt_count * NI, NJ * virtuals)
    cycle_part = jnp.dot(cycle_amps, panel, precision=precise, preferred_element_type=jnp.float32)
    partial_value = lax.psum_scatter(ladder_terms, "col", scatter_dimension=1, tiled=True)
    ladder = lax.psum_scatter(partial_value, "exc", scatter_dimension=0, tiled=True)
    cycle = lax.psum_scatter(cycle_part, ("grp", "exc"), scatter_dimension=0, tiled=True)
    return ladder + cycle


def cycle_kernel(place, amps_ref, panel_ref, out_ref, total):
    step = pl.program_id(0)

    @pl.when(step == 0)
    def _():
        total[...] = jnp.zeros_like(total)

    high, low = split(amps_ref[...])
    panel_high, panel_low = split(panel_ref[...])
    rows = high.shape[0]
    both = dot(jnp.concatenate([high, low], axis=0), panel_high)
    total[...] += both[:rows] + both[rows:] + dot(high, panel_low)

    @pl.when(step == pl.num_programs(0) - 1)
    def _():
        for slot in range(rows // NI):
            row = (place[0] ^ slot) * NI
            for i in range(NI):
                out_ref[slot, pl.ds(i, 1), :] = total[pl.ds(row + i, 1), :]


def cycle_slots(place, cycle_amps, panel):
    rows, depth = cycle_amps.shape
    columns = panel.shape[1]
    block = min(512, depth)
    return pl.pallas_call(
        cycle_kernel,
        out_shape=jax.ShapeDtypeStruct((rows // NI, NI, columns), jnp.float32),
        grid_spec=pltpu.PrefetchScalarGridSpec(
            num_scalar_prefetch=1,
            grid=(depth // block,),
            in_specs=[
                pl.BlockSpec((rows, block), lambda s, place: (0, s)),
                pl.BlockSpec((block, columns), lambda s, place: (s, 0)),
            ],
            out_specs=pl.BlockSpec((rows // NI, NI, columns), lambda s, place: (0, 0, 0)),
            scratch_shapes=[pltpu.VMEM((rows, columns), jnp.float32)],
        ),
        compiler_params=pltpu.CompilerParams(vmem_limit_bytes=VMEM_BYTES),
        cost_estimate=pl.CostEstimate(
            flops=6 * rows * depth * columns, bytes_accessed=4 * depth * columns, transcendentals=0
        ),
    )(place, cycle_amps, panel)


DEPTH = 16
GROUP = 4


def ladder_kernel(place, own_ref, other_ref, amp_ref, fitted_ref, keep_ref, send_ref,
                  amp_high, amp_low, rows_ref, left, total):
    step = pl.program_id(0)
    steps = pl.num_programs(0)
    pairs, fit_count, virtuals = amp_ref.shape
    a_count = own_ref.shape[1]
    core, exc, col = place[1], place[2], place[3]
    half = 2 * a_count * pairs // 2
    m = 2 * a_count * pairs

    @pl.when(step == 0)
    def _():
        total[...] = jnp.zeros_like(total)
        for pair in range(pairs):
            high, low = split(amp_ref[pair])
            amp_high[pl.ds(pair * fit_count, fit_count), :] = high
            amp_low[pl.ds(pair * fit_count, fit_count), :] = low

    @pl.when(step % GROUP == 0)
    def _():
        count = DEPTH * GROUP
        first = (core * steps + step) * DEPTH
        for p in range(count):
            rows_ref[pl.ds(2 * a_count * p, a_count), :] = own_ref[first + p]
            rows_ref[pl.ds(2 * a_count * p + a_count, a_count), :] = other_ref[first + p]
        high, low = split(rows_ref[...])
        stacked = jnp.concatenate([high, low], axis=0)
        n_rows = high.shape[0]
        upper = lax.broadcasted_iota(jnp.int32, (n_rows // 8, 8, LANES), 1) < 4

        for quad in range(pairs // 4):
            lanes = pl.ds(quad * 4 * fit_count, 4 * fit_count)
            weights = amp_high[lanes, :]
            both = dot_t(stacked, weights)
            product = both[:n_rows] + both[n_rows:] + dot_t(high, amp_low[lanes, :])
            for odd in range(2):
                tiles = []
                for duo in range(2):
                    one = product[:, (2 * duo) * LANES : (2 * duo + 1) * LANES].reshape(n_rows // 8, 8, LANES)
                    two = product[:, (2 * duo + 1) * LANES : (2 * duo + 2) * LANES].reshape(n_rows // 8, 8, LANES)
                    if odd:
                        tiles.append(jnp.where(upper, pltpu.roll(one, 4, 1), two))
                    else:
                        tiles.append(jnp.where(upper, one, pltpu.roll(two, 4, 1)))
                tile_high, tile_low = split(jnp.concatenate(tiles, axis=1))
                for index in range(n_rows // 8):
                    slot, place_in = divmod(2 * index + odd, DEPTH)
                    left[slot, pl.ds(16 * quad, 16), pl.ds(place_in * LANES, LANES)] = tile_high[index]
                    left[slot, pl.ds(m + 16 * quad, 16), pl.ds(place_in * LANES, LANES)] = tile_low[index]

    slot = step % GROUP
    part = 4
    for piece in range(DEPTH // part):
        fitted = fitted_ref[pl.ds(piece * part, part)].reshape(part * fit_count, virtuals)
        fitted_high, fitted_low = split(fitted)
        lanes = pl.ds(piece * part * LANES, part * LANES)
        both = dot(left[slot, :, lanes], fitted_high)
        total[...] += both[:m] + both[m:] + dot(left[slot, pl.ds(0, m), lanes], fitted_low)

    @pl.when(step == steps - 1)
    def _():
        cols = NJ // 2
        for target, out in ((0, keep_ref), (1, send_ref)):
            for far in range(2):
                for away in range(cols):
                    for i in range(NI):
                        for j in range(2):
                            pair = i * NJ + (col ^ away) * 2 + j
                            row = pair * 2 * a_count + target * a_count + (exc ^ far)
                            out[far, pl.ds(away * NI + i, 1), pl.ds(j * virtuals, virtuals)] = total[pl.ds(row, 1), :]


def ladder_slots(place, own, other, pair_amps, fitted_factor):
    pairs, fit_count, virtuals = pair_amps.shape
    aux_count, a_count = own.shape[:2]
    steps = aux_count // 2 // DEPTH
    m = 2 * a_count * pairs
    whole = lambda *shape: pl.BlockSpec(shape, lambda s, place: (0,) * len(shape), pipeline_mode=pl.Buffered(1))
    out = jax.ShapeDtypeStruct((2, NJ, 2 * virtuals), jnp.float32)
    out_spec = pl.BlockSpec(out.shape, lambda s, place: (0, 0, 0))
    return pl.pallas_call(
        ladder_kernel,
        out_shape=(out, out),
        grid_spec=pltpu.PrefetchScalarGridSpec(
            num_scalar_prefetch=1,
            grid=(steps,),
            in_specs=[
                whole(*own.shape),
                whole(*own.shape),
                whole(*pair_amps.shape),
                pl.BlockSpec((DEPTH, fit_count, virtuals), lambda s, place: (place[1] * steps + s, 0, 0)),
            ],
            out_specs=(out_spec, out_spec),
            scratch_shapes=[
                pltpu.VMEM((pairs * fit_count, virtuals), jnp.bfloat16),
                pltpu.VMEM((pairs * fit_count, virtuals), jnp.bfloat16),
                pltpu.VMEM((DEPTH * GROUP * 2 * a_count, virtuals), jnp.float32),
                pltpu.VMEM((GROUP, 2 * m, DEPTH * LANES), jnp.bfloat16),
                pltpu.VMEM((m, virtuals), jnp.float32),
            ],
        ),
        compiler_params=pltpu.CompilerParams(vmem_limit_bytes=VMEM_BYTES),
        cost_estimate=pl.CostEstimate(
            flops=6 * aux_count * a_count * pairs * fit_count * virtuals * 2,
            bytes_accessed=2 * aux_count * fit_count * virtuals, transcendentals=0
        ),
    )(place, own, other, pair_amps, fitted_factor)


def swap(x, axis, size, bit):
    return lax.ppermute(x, axis, [(n, n ^ bit) for n in range(size)])


def fast(grp_count, exc_count, col_count, window_factor, fitted_factor, pair_amps, cycle_amps, panel):
    grp, exc, col = lax.axis_index("grp"), lax.axis_index("exc"), lax.axis_index("col")
    place = jnp.stack([grp * exc_count + exc, grp % 2, exc, col]).astype(jnp.int32)
    other = swap(window_factor, "grp", grp_count, 1)
    cycle = cycle_slots(place, cycle_amps, panel)
    cycle_far = swap(cycle[4:], "grp", grp_count, 2)
    keep, send = ladder_slots(place, window_factor, other, pair_amps, fitted_factor)
    near = cycle[:4] + cycle_far
    near = near.reshape(2, 2, NI, -1)
    send = send.at[:, :NI].add(near[1])
    keep = keep.at[:, :NI].add(near[0])
    total = keep + swap(send, "grp", grp_count, 1)
    total = total[0] + swap(total[1], "exc", exc_count, 1)
    bit = col_count // 2
    while bit:
        total = total[: bit * NI] + swap(total[bit * NI :], "col", col_count, bit)
        bit //= 2
    return total


def solution(mesh):
    placed = (
        P("exc", "grp", None),
        P("exc", "col", None),
        P(None, "col", None),
        P(None, ("grp", "exc")),
        P(("grp", "exc"), "col"),
    )
    grp_count, exc_count, col_count = (mesh.shape[name] for name in ("grp", "exc", "col"))

    def shards(window_factor, fitted_factor, pair_amps, cycle_amps, panel):
        aux_count, a_count, virtuals = window_factor.shape
        fits = (
            grp_count == 4
            and exc_count == 2
            and a_count == 2
            and 2 * col_count == NJ
            and fitted_factor.shape[1] == LANES
            and virtuals % LANES == 0
            and aux_count % (2 * DEPTH * GROUP) == 0
        )
        body = functools.partial(fast, grp_count, exc_count, col_count) if fits else plain
        return body(window_factor, fitted_factor, pair_amps, cycle_amps, panel)

    return jax.shard_map(
        shards, mesh=mesh, in_specs=placed, out_specs=P(("grp", "exc"), "col"), check_vma=False
    )
```

time: 198 us -> 75.9 us (0.38)
  matrix products: 114 us -> 0 us
  Pallas kernels: 0 us -> 49.9 us
  waiting for transfers between devices: 42.9 us -> 9.06 us
  between operations: 16.2 us -> 0.04 us
  local copies, waits for them, and re-layouts: 14.8 us -> 2.12 us
  starting transfers between devices: 0.05 us -> 9.86 us
  blocking collectives: 8.23 us -> 0 us
  other arithmetic: 1.36 us -> 4.33 us
    dot_general x3 -> x0, matrix products: 114 us -> none  [the longest x1 84.2 us: shards(): jnp.dot(inner_rows, fitted_rows, precision=precise, preferred_element_typ...]
    pallas_call x0 -> x2, Pallas kernels: none -> 49.9 us  [the longest x1 39.2 us: ladder_slots(): pl.pallas_call(ladder_kernel, out_shape=(out, out), grid_spec=pltpu.Prefe...]
    unnamed x4 -> x0, waiting for transfers between devices: 42.9 us -> none
    ppermute x0 -> x6, starting transfers between devices: none -> 9.86 us  [swap(): return lax.ppermute(x, axis, [(n, n ^ bit) for n in range(size)])]
    ppermute x0 -> x6, waiting for transfers between devices: none -> 9.06 us  [swap(): return lax.ppermute(x, axis, [(n, n ^ bit) for n in range(size)])]
    transpose x1 -> x0, local copies, waits for them, and re-layouts: 8.69 us -> none  [shards(): jnp.einsum('pac,ijdc->aijpd', window_factor, amplitude, precision=precise)]
    unnamed x1 -> x0, blocking collectives: 8.23 us -> none
    unnamed x12 -> x2, local copies, waits for them, and re-layouts: 6.07 us -> 1.34 us
  transfers between devices with their start and end apart: 2 -> 6, of which waited for: 2 -> 5; matrix products, arithmetic and copies ran while one was open for 7% -> 3% of each run, Pallas kernels for 0% -> 14%
where the time goes in v1:
time: 75.9 us; the launch traced here: 75.3 us
  Pallas kernels  49.9 us (66%)
  starting transfers between devices  9.86 us (13%)
  waiting for transfers between devices  9.06 us (12%)
  other arithmetic  4.33 us (6%)
  local copies, waits for them, and re-layouts  2.12 us (3%)
    pallas_call x1, Pallas kernels, ladder_slots(): pl.pallas_call(ladder_kernel, out_shape=(out, out), grid_spec=pltpu.Prefe...  39.2 us
    pallas_call x1, Pallas kernels, cycle_slots(): pl.pallas_call(cycle_kernel, out_shape=jax.ShapeDtypeStruct((rows // NI,...  10.7 us
    ppermute x6, starting transfers between devices, swap(): return lax.ppermute(x, axis, [(n, n ^ bit) for n in range(size)])  9.86 us
    ppermute x6, waiting for transfers between devices, swap(): return lax.ppermute(x, axis, [(n, n ^ bit) for n in range(size)])  9.06 us
  transfers between devices with their start and end apart: 6, of which 5 were waited for; matrix products, arithmetic and copies ran while one was open for 3% of the time, Pallas kernels for 14%

profile of v1, /device:TPU:0, one launch (start us, length us, event | category | flops | bytes accessed | tf_op | source)
XLA Modules:
  0.0 75.3 jit_solution(7449430617993024590)
XLA Ops:
  0.0 0.5 collective-permute-start
  0.5 0.6 pad_add_fusion.place
  1.1 10.7 %shard_map.56 = f32[8,2,1024]{2,1,0:T(2,128)} custom-call(s32[4]{0:T(128)} %pad_add_fusion.place, f32[16,4096]{1,0:T(8,128)} %amps_ref.1, f32[4096,1024]{1,0:T(8,128)} %panel_ref.1), custom_call_target="tpu_custom_call" | custom-call | flops 402653184 | bytes 16777216 | tf_op jit(solution)/shard_map/pallas_call | solution.py:72
  11.7 0.8 %slice.93 = f32[4,2,1024]{2,1,0:T(2,128)S(1)} slice(f32[8,2,1024]{2,1,0:T(2,128)} %shard_map.56), slice={[4:8], [0:2], [0:1024]} | slice | bytes 65536 | tf_op jit(solution)/shard_map/slice | solution.py:214
  12.5 2.5 %collective-permute-start.1 = (f32[4,2,1024]{2,1,0:T(2,128)S(1)}, f32[4,2,1024]{2,1,0:T(2,128)S(1)}, u32[]{:S(2)}, u32[]{:S(2)}) collective-permute-start(f32[4,2,1024]{2,1,0:T(2,128)S(1)} %slice.93), channel_id=1, source_target_pairs={{0,16},{8,24},{16,0},{24,8},{1,17},{9,25},{17,1},{25,9},{2,18},{10... | collective-permute-start | bytes 98312 | tf_op jit(solution)/shard_map/ppermute | solution.py:206
  15.0 2.1 %collective-permute-done.1 = f32[4,2,1024]{2,1,0:T(2,128)S(1)} collective-permute-done((f32[4,2,1024]{2,1,0:T(2,128)S(1)}, f32[4,2,1024]{2,1,0:T(2,128)S(1)}, u32[]{:S(2)}, u32[]{:S(2)}) %collective-permute-start.1) | collective-permute-done | bytes 32800 | tf_op jit(solution)/shard_map/ppermute | solution.py:206
  17.1 0.8 %slice_add_fusion = f32[4,2,1024]{2,1,0:T(2,128)S(1)} fusion(f32[4,2,1024]{2,1,0:T(2,128)S(1)} %collective-permute-done.1, f32[8,2,1024]{2,1,0:T(2,128)} %shard_map.56), kind=kLoop, calls=%fused_computation.3 | loop fusion | flops 8192 | bytes 98304 | tf_op jit(solution)/shard_map/add | solution.py:216
  17.8 0.0 collective-permute-done.other_ref
  17.8 0.0 copy-start
  17.9 1.3 %copy-done = f32[512,2,512]{2,1,0:T(2,128)} copy-done((f32[512,2,512]{2,1,0:T(2,128)}, f32[512,2,512]{2,1,0:T(2,128)S(1)}, u32[]{:S(2)}) %copy-start) | copy-done | bytes 2097176
  19.2 39.2 %shard_map.55 = (f32[2,8,1024]{2,1,0:T(8,128)}, f32[2,8,1024]{2,1,0:T(8,128)}) custom-call(s32[4]{0:T(128)} %pad_add_fusion.place, f32[512,2,512]{2,1,0:T(2,128)} %own_ref.1, f32[512,2,512]{2,1,0:T(2,128)} %copy-done, f32[16,128,512]{2,1,0:T(8,128)} %amp_ref.1, f32[512,128,512]{2,1,0:T(8,128)} %fitted_ref.1), custom_call_target="tpu_custom_call" | custom-call | flops 12884901888 | bytes 67108864 | tf_op jit(solution)/shard_map/pallas_call | solution.py:176
  58.4 1.5 %fusion.1 = (f32[2,8,1024]{2,1,0:T(8,128)}, f32[2,8,1024]{2,1,0:T(8,128)}) fusion(f32[2,8,1024]{2,1,0:T(8,128)} %get-tuple-element.32, f32[4,2,1024]{2,1,0:T(2,128)S(1)} %slice_add_fusion, f32[2,8,1024]{2,1,0:T(8,128)} %get-tuple-element.31), kind=kLoop, calls=%fused_computation.6 | loop fusion | flops 8192 | bytes 98304 | tf_op jit(solution)/shard_map/scatter-add | solution.py:218
  59.9 0.0 collective-permute-start.2
  59.9 1.5 %collective-permute-done.2 = f32[2,8,1024]{2,1,0:T(8,128)S(1)} collective-permute-done((f32[2,8,1024]{2,1,0:T(8,128)}, f32[2,8,1024]{2,1,0:T(8,128)S(1)}, u32[]{:S(2)}, u32[]{:S(2)}) %collective-permute-start.2) | collective-permute-done | bytes 65568 | tf_op jit(solution)/shard_map/ppermute | solution.py:206
  61.3 0.8 %add.41 = f32[2,8,1024]{2,1,0:T(8,128)S(1)} add(f32[2,8,1024]{2,1,0:T(8,128)} %get-tuple-element.34, f32[2,8,1024]{2,1,0:T(8,128)S(1)} %collective-permute-done.2) | non-fusion elementwise | flops 16384 | bytes 196608 | tf_op jit(solution)/shard_map/add | solution.py:220
  62.2 1.9 %collective-permute-start.3 = (f32[8,1024]{1,0:T(8,128)S(1)}, f32[8,1024]{1,0:T(8,128)S(1)}, u32[]{:S(2)}, u32[]{:S(2)}) collective-permute-start(f32[8,1024]{1,0:T(8,128)S(1)} %slice_bitcast_fusion), channel_id=1, source_target_pairs={{0,4},{4,0},{1,5},{5,1},{2,6},{6,2},{3,7},{7,3},{8,12},{12,8},{9,1... | collective-permute-start | bytes 98312 | tf_op jit(solution)/shard_map/ppermute | solution.py:206
  64.1 2.1 %collective-permute-done.3 = f32[8,1024]{1,0:T(8,128)S(1)} collective-permute-done((f32[8,1024]{1,0:T(8,128)S(1)}, f32[8,1024]{1,0:T(8,128)S(1)}, u32[]{:S(2)}, u32[]{:S(2)}) %collective-permute-start.3) | collective-permute-done | bytes 32800 | tf_op jit(solution)/shard_map/ppermute | solution.py:206
  66.2 3.0 %collective-permute-start.4 = (f32[4,1024]{1,0:T(4,128)S(1)}, f32[4,1024]{1,0:T(4,128)S(1)}, u32[]{:S(2)}, u32[]{:S(2)}) collective-permute-start(f32[4,1024]{1,0:T(4,128)S(1)} %slice.99), channel_id=1, source_target_pairs={{0,2},{1,3},{2,0},{3,1},{4,6},{5,7},{6,4},{7,5},{8,10},{9,11},{10,... | collective-permute-start | bytes 49160 | tf_op jit(solution)/shard_map/ppermute | solution.py:206
  69.2 1.7 %collective-permute-done.4 = f32[4,1024]{1,0:T(4,128)S(1)} collective-permute-done((f32[4,1024]{1,0:T(4,128)S(1)}, f32[4,1024]{1,0:T(4,128)S(1)}, u32[]{:S(2)}, u32[]{:S(2)}) %collective-permute-start.4) | collective-permute-done | bytes 16416 | tf_op jit(solution)/shard_map/ppermute | solution.py:206
  70.9 2.0 %collective-permute-start.5 = (f32[2,1024]{1,0:T(2,128)S(1)}, f32[2,1024]{1,0:T(2,128)S(1)}, u32[]{:S(2)}, u32[]{:S(2)}) collective-permute-start(f32[2,1024]{1,0:T(2,128)S(1)} %slice.101), channel_id=1, source_target_pairs={{0,1},{1,0},{2,3},{3,2},{4,5},{5,4},{6,7},{7,6},{8,9},{9,8},{10,11... | collective-permute-start | bytes 24584 | tf_op jit(solution)/shard_map/ppermute | solution.py:206
  72.9 1.8 %collective-permute-done.5 = f32[2,1024]{1,0:T(2,128)S(1)} collective-permute-done((f32[2,1024]{1,0:T(2,128)S(1)}, f32[2,1024]{1,0:T(2,128)S(1)}, u32[]{:S(2)}, u32[]{:S(2)}) %collective-permute-start.5) | collective-permute-done | bytes 8224 | tf_op jit(solution)/shard_map/ppermute | solution.py:206
  74.7 0.6 slice_add_fusion.4
  (5 shorter events, 0.0 us)
Async XLA Ops:
  0.0 17.8 %collective-permute-start = (f32[512,2,512]{2,1,0:T(2,128)}, f32[512,2,512]{2,1,0:T(2,128)S(1)}, u32[]{:S(2)}, u32[]{:S(2)}) collective-permute-start(f32[512,2,512]{2,1,0:T(2,128)} %own_ref.1), channel_id=1, source_target_pairs={{0,8},{8,0},{16,24},{24,16},{1,9},{9,1},{17,25},{25,17},{2,10},{10... | collective-permute-start | bytes 6291464 | tf_op jit(solution)/shard_map/ppermute | solution.py:206
  12.5 4.6 %collective-permute-start.1 = (f32[4,2,1024]{2,1,0:T(2,128)S(1)}, f32[4,2,1024]{2,1,0:T(2,128)S(1)}, u32[]{:S(2)}, u32[]{:S(2)}) collective-permute-start(f32[4,2,1024]{2,1,0:T(2,128)S(1)} %slice.93), channel_id=1, source_target_pairs={{0,16},{8,24},{16,0},{24,8},{1,17},{9,25},{17,1},{25,9},{2,18},{10... | collective-permute-start | bytes 98312 | tf_op jit(solution)/shard_map/ppermute | solution.py:206
  17.8 1.3 %copy-start = (f32[512,2,512]{2,1,0:T(2,128)}, f32[512,2,512]{2,1,0:T(2,128)S(1)}, u32[]{:S(2)}) copy-start(f32[512,2,512]{2,1,0:T(2,128)S(1)} %collective-permute-done.other_ref) | copy-start | bytes 6291460
  59.9 1.5 %collective-permute-start.2 = (f32[2,8,1024]{2,1,0:T(8,128)}, f32[2,8,1024]{2,1,0:T(8,128)S(1)}, u32[]{:S(2)}, u32[]{:S(2)}) collective-permute-start(f32[2,8,1024]{2,1,0:T(8,128)} %get-tuple-element.33), channel_id=1, source_target_pairs={{0,8},{8,0},{16,24},{24,16},{1,9},{9,1},{17,25},{25,17},{2,10},{10... | collective-permute-start | bytes 196616 | tf_op jit(solution)/shard_map/ppermute | solution.py:206
  62.2 4.0 %collective-permute-start.3 = (f32[8,1024]{1,0:T(8,128)S(1)}, f32[8,1024]{1,0:T(8,128)S(1)}, u32[]{:S(2)}, u32[]{:S(2)}) collective-permute-start(f32[8,1024]{1,0:T(8,128)S(1)} %slice_bitcast_fusion), channel_id=1, source_target_pairs={{0,4},{4,0},{1,5},{5,1},{2,6},{6,2},{3,7},{7,3},{8,12},{12,8},{9,1... | collective-permute-start | bytes 98312 | tf_op jit(solution)/shard_map/ppermute | solution.py:206
  66.2 4.8 %collective-permute-start.4 = (f32[4,1024]{1,0:T(4,128)S(1)}, f32[4,1024]{1,0:T(4,128)S(1)}, u32[]{:S(2)}, u32[]{:S(2)}) collective-permute-start(f32[4,1024]{1,0:T(4,128)S(1)} %slice.99), channel_id=1, source_target_pairs={{0,2},{1,3},{2,0},{3,1},{4,6},{5,7},{6,4},{7,5},{8,10},{9,11},{10,... | collective-permute-start | bytes 49160 | tf_op jit(solution)/shard_map/ppermute | solution.py:206
  70.9 3.7 %collective-permute-start.5 = (f32[2,1024]{1,0:T(2,128)S(1)}, f32[2,1024]{1,0:T(2,128)S(1)}, u32[]{:S(2)}, u32[]{:S(2)}) collective-permute-start(f32[2,1024]{1,0:T(2,128)S(1)} %slice.101), channel_id=1, source_target_pairs={{0,1},{1,0},{2,3},{3,2},{4,5},{5,4},{6,7},{7,6},{8,9},{9,8},{10,11... | collective-permute-start | bytes 24584 | tf_op jit(solution)/shard_map/ppermute | solution.py:206

commit v2 on v0

v2 whole, which is shorter than its diff:
```python
import functools

import jax
import jax.numpy as jnp
from jax import lax
from jax.experimental import pallas as pl
from jax.experimental.pallas import tpu as pltpu
from jax.sharding import PartitionSpec as P

NI = 2
NJ = 8
VMEM_BYTES = 56 * 1024 * 1024
LANES = 128


def split(x):
    high = x.astype(jnp.bfloat16)
    low = (x - high.astype(jnp.float32)).astype(jnp.bfloat16)
    return high, low


def dot(x, y):
    return jnp.dot(x, y, preferred_element_type=jnp.float32)


def dot_t(x, y):
    return lax.dot_general(x, y, (((1,), (1,)), ((), ())), preferred_element_type=jnp.float32)


def plain(window_factor, fitted_factor, pair_amps, cycle_amps, panel):
    precise = lax.Precision.HIGHEST
    aux_count, virt_count, virtuals = window_factor.shape
    fit_count = fitted_factor.shape[1]
    amplitude = pair_amps.reshape(NI, NJ, fit_count, virtuals)
    inner = jnp.einsum("pac,ijdc->aijpd", window_factor, amplitude, precision=precise)
    inner_rows = inner.reshape(virt_count * NI * NJ, aux_count * fit_count)
    fitted_rows = fitted_factor.reshape(aux_count * fit_count, virtuals)
    ladder_terms = jnp.dot(inner_rows, fitted_rows, precision=precise, preferred_element_type=jnp.float32)
    ladder_terms = ladder_terms.reshape(virt_count * NI, NJ * virtuals)
    cycle_part = jnp.dot(cycle_amps, panel, precision=precise, preferred_element_type=jnp.float32)
    partial_value = lax.psum_scatter(ladder_terms, "col", scatter_dimension=1, tiled=True)
    ladder = lax.psum_scatter(partial_value, "exc", scatter_dimension=0, tiled=True)
    cycle = lax.psum_scatter(cycle_part, ("grp", "exc"), scatter_dimension=0, tiled=True)
    return ladder + cycle


STRIP = 512
STRIPS = 3


def cycle_kernel(amps_hbm, panel_ref, near_ref, far_ref, across_ref, amps_ref, strips, total, sems, amps_sem):
    rows, depth = amps_ref.shape
    count = depth // STRIP
    me = lax.axis_index("grp") * lax.axis_size("exc") + lax.axis_index("exc")
    amps_copy = pltpu.make_async_copy(amps_hbm, amps_ref, amps_sem)
    amps_copy.start()

    def fetch(n):
        return pltpu.make_async_copy(panel_ref.at[pl.ds(n * STRIP, STRIP)], strips.at[n], sems.at[n])

    for n in range(min(STRIPS, count)):
        fetch(n).start()
    total[...] = jnp.zeros_like(total)
    amps_copy.wait()
    for n in range(count):
        fetch(n).wait()
        if n + STRIPS < count:
            fetch(n + STRIPS).start()
        high, low = split(amps_ref[:, n * STRIP : (n + 1) * STRIP])
        panel_high, panel_low = split(strips[n])
        both = dot(jnp.concatenate([high, low], axis=0), panel_high)
        total[...] += both[:rows] + both[rows:] + dot(high, panel_low)
    exc_count = lax.axis_size("exc")
    outs = [(near_ref, n) for n in range(2 * exc_count)]
    outs += [(ref, n) for ref in (far_ref, across_ref) for n in range(exc_count)]
    for slot, (out, n) in enumerate(outs):
        row = (me ^ slot) * NI
        for i in range(NI):
            out[n, pl.ds(i, 1), :] = total[pl.ds(row + i, 1), :]


def cycle_slots(cycle_amps, panel):
    rows, depth = cycle_amps.shape
    columns = panel.shape[1]
    near = jax.ShapeDtypeStruct((rows // NI // 2, NI, columns), jnp.float32)
    far = jax.ShapeDtypeStruct((rows // NI // 4, NI, columns), jnp.float32)
    return pl.pallas_call(
        cycle_kernel,
        out_shape=(near, far, far),
        in_specs=[pl.BlockSpec(memory_space=pltpu.HBM)] * 2,
        out_specs=(pl.BlockSpec(memory_space=pltpu.VMEM),) * 3,
        scratch_shapes=[
            pltpu.VMEM((rows, depth), jnp.float32),
            pltpu.VMEM((depth // STRIP, STRIP, columns), jnp.float32),
            pltpu.VMEM((rows, columns), jnp.float32),
            pltpu.SemaphoreType.DMA((depth // STRIP,)),
            pltpu.SemaphoreType.DMA,
        ],
        compiler_params=pltpu.CompilerParams(vmem_limit_bytes=VMEM_BYTES),
        cost_estimate=pl.CostEstimate(
            flops=6 * rows * depth * columns, bytes_accessed=4 * depth * columns, transcendentals=0
        ),
    )(cycle_amps, panel)


DEPTH = 16
GROUP = 4
SLOTS = 6
PART = 2


def ladder_kernel(own_hbm, other_hbm, amp_hbm, fitted_hbm, near_ref, keep_ref, send_ref,
                  own, other, amp, amp_high, amp_low, rows_ref, left, fitted_in, total, sems, fitted_sems):
    pairs, fit_count, virtuals = amp_hbm.shape
    aux_half, a_count = own.shape[:2]
    steps = aux_half // DEPTH
    core, exc, col = lax.axis_index("grp") % 2, lax.axis_index("exc"), lax.axis_index("col")
    first = core * aux_half
    m = 2 * a_count * pairs

    def fetch(step, slot):
        source = fitted_hbm.at[pl.ds(first + step * DEPTH, DEPTH)]
        return pltpu.make_async_copy(source, fitted_in.at[slot], fitted_sems.at[slot])

    small = [
        pltpu.make_async_copy(amp_hbm, amp, sems.at[0]),
        pltpu.make_async_copy(own_hbm.at[pl.ds(first, aux_half)], own, sems.at[1]),
        pltpu.make_async_copy(other_hbm.at[pl.ds(first, aux_half)], other, sems.at[2]),
    ]
    for copy in small:
        copy.start()
    fetch(0, 0).start()
    total[...] = jnp.zeros_like(total)
    small[0].wait()
    fetch(1, 1).start()
    for pair in range(pairs):
        high, low = split(amp[pair])
        amp_high[pl.ds(pair * fit_count, fit_count), :] = high
        amp_low[pl.ds(pair * fit_count, fit_count), :] = low
    small[1].wait()
    small[2].wait()
    for step in range(2, SLOTS):
        fetch(step, step).start()

    def first_product(group):
        count = DEPTH * GROUP
        for p in range(count):
            rows_ref[pl.ds(2 * a_count * p, a_count), :] = own[group * count + p]
            rows_ref[pl.ds(2 * a_count * p + a_count, a_count), :] = other[group * count + p]
        high, low = split(rows_ref[...])
        stacked = jnp.concatenate([high, low], axis=0)
        n_rows = high.shape[0]
        upper = lax.broadcasted_iota(jnp.int32, (n_rows // 8, 8, LANES), 1) < 4

        for quad in range(pairs // 4):
            lanes = pl.ds(quad * 4 * fit_count, 4 * fit_count)
            both = dot_t(stacked, amp_high[lanes, :])
            product = both[:n_rows] + both[n_rows:] + dot_t(high, amp_low[lanes, :])
            for odd in range(2):
                tiles = []
                for duo in range(2):
                    one = product[:, (2 * duo) * LANES : (2 * duo + 1) * LANES].reshape(n_rows // 8, 8, LANES)
                    two = product[:, (2 * duo + 1) * LANES : (2 * duo + 2) * LANES].reshape(n_rows // 8, 8, LANES)
                    if odd:
                        tiles.append(jnp.where(upper, pltpu.roll(one, 4, 1), two))
                    else:
                        tiles.append(jnp.where(upper, one, pltpu.roll(two, 4, 1)))
                tile_high, tile_low = split(jnp.concatenate(tiles, axis=1))
                for index in range(n_rows // 8):
                    slot, place_in = divmod(2 * index + odd, DEPTH)
                    left[slot, pl.ds(16 * quad, 16), pl.ds(place_in * LANES, LANES)] = tile_high[index]
                    left[slot, pl.ds(m + 16 * quad, 16), pl.ds(place_in * LANES, LANES)] = tile_low[index]

    @pl.loop(0, steps // GROUP)
    def _(group):
        first_product(group)
        for near in range(GROUP):
            step = group * GROUP + near
            slot = lax.rem(step, SLOTS)
            fetch(step, slot).wait()
            for piece in range(DEPTH // PART):
                fitted = fitted_in[slot, pl.ds(piece * PART, PART)].reshape(PART * fit_count, virtuals)
                fitted_high, fitted_low = split(fitted)
                lanes = pl.ds(piece * PART * LANES, PART * LANES)
                both = dot(left[near, :, lanes], fitted_high)
                total[...] += both[:m] + both[m:] + dot(left[near, pl.ds(0, m), lanes], fitted_low)

            @pl.when(step + SLOTS < steps)
            def _():
                fetch(step + SLOTS, slot).start()

    for target, out in ((0, keep_ref), (1, send_ref)):
        for far in range(2):
            for away in range(NJ // 2):
                for i in range(NI):
                    for j in range(2):
                        pair = i * NJ + (col ^ away) * 2 + j
                        row = pair * 2 * a_count + target * a_count + (exc ^ far)
                        columns = pl.ds(j * virtuals, virtuals)
                        value = total[pl.ds(row, 1), :]
                        if away == 0:
                            value += near_ref[target * 2 + far, pl.ds(i, 1), columns]
                        out[far, pl.ds(away * NI + i, 1), columns] = value


def ladder_slots(own, other, pair_amps, fitted_factor, near):
    pairs, fit_count, virtuals = pair_amps.shape
    aux_count, a_count = own.shape[:2]
    m = 2 * a_count * pairs
    out = jax.ShapeDtypeStruct((2, NJ, 2 * virtuals), jnp.float32)
    half = (aux_count // 2, a_count, virtuals)
    return pl.pallas_call(
        ladder_kernel,
        out_shape=(out, out),
        in_specs=[
            pl.BlockSpec(memory_space=pltpu.HBM),
            pl.BlockSpec(memory_space=pl.ANY),
            pl.BlockSpec(memory_space=pltpu.HBM),
            pl.BlockSpec(memory_space=pltpu.HBM),
            pl.BlockSpec(memory_space=pltpu.VMEM),
        ],
        out_specs=(pl.BlockSpec(memory_space=pltpu.VMEM),) * 2,
        scratch_shapes=[
            pltpu.VMEM(half, jnp.float32),
            pltpu.VMEM(half, jnp.float32),
            pltpu.VMEM(pair_amps.shape, jnp.float32),
            pltpu.VMEM((pairs * fit_count, virtuals), jnp.bfloat16),
            pltpu.VMEM((pairs * fit_count, virtuals), jnp.bfloat16),
            pltpu.VMEM((DEPTH * GROUP * 2 * a_count, virtuals), jnp.float32),
            pltpu.VMEM((GROUP, 2 * m, DEPTH * LANES), jnp.bfloat16),
            pltpu.VMEM((SLOTS, DEPTH, fit_count, virtuals), jnp.float32),
            pltpu.VMEM((m, virtuals), jnp.float32),
            pltpu.SemaphoreType.DMA((3,)),
            pltpu.SemaphoreType.DMA((SLOTS,)),
        ],
        compiler_params=pltpu.CompilerParams(vmem_limit_bytes=VMEM_BYTES),
        cost_estimate=pl.CostEstimate(
            flops=6 * aux_count * a_count * pairs * fit_count * virtuals * 2,
            bytes_accessed=2 * aux_count * fit_count * virtuals, transcendentals=0
        ),
    )(own, other, pair_amps, fitted_factor, near)


def swap(x, axis, size, bit):
    return lax.ppermute(x, axis, [(n, n ^ bit) for n in range(size)])


def fast(grp_count, exc_count, col_count, window_factor, fitted_factor, pair_amps, cycle_amps, panel):
    other = swap(window_factor, "grp", grp_count, 1)
    near, far, across = cycle_slots(cycle_amps, panel)
    one, two = swap(far, "grp", grp_count, 2), swap(across, "grp", grp_count, 3)
    keep, send = ladder_slots(window_factor, other, pair_amps, fitted_factor, near)
    keep, send, one, two = lax.optimization_barrier((keep, send, one, two))
    total = (keep + swap(send, "grp", grp_count, 1)).at[:, :NI].add(one + two)
    total = total[0] + swap(total[1], "exc", exc_count, 1)
    bit = col_count // 2
    while bit:
        total = total[: bit * NI] + swap(total[bit * NI :], "col", col_count, bit)
        bit //= 2
    return total


def solution(mesh):
    placed = (
        P("exc", "grp", None),
        P("exc", "col", None),
        P(None, "col", None),
        P(None, ("grp", "exc")),
        P(("grp", "exc"), "col"),
    )
    grp_count, exc_count, col_count = (mesh.shape[name] for name in ("grp", "exc", "col"))

    def shards(window_factor, fitted_factor, pair_amps, cycle_amps, panel):
        aux_count, a_count, virtuals = window_factor.shape
        fits = (
            grp_count == 4
            and exc_count == 2
            and a_count == 2
            and 2 * col_count == NJ
            and fitted_factor.shape[1] == LANES
            and virtuals % LANES == 0
            and aux_count % (2 * DEPTH * GROUP) == 0
            and cycle_amps.shape[1] % STRIP == 0
        )
        body = functools.partial(fast, grp_count, exc_count, col_count) if fits else plain
        return body(window_factor, fitted_factor, pair_amps, cycle_amps, panel)

    return jax.shard_map(
        shards, mesh=mesh, in_specs=placed, out_specs=P(("grp", "exc"), "col"), check_vma=False
    )
```

time: 198 us -> 53.3 us (0.27)
  matrix products: 114 us -> 0 us
  waiting for transfers between devices: 42.9 us -> 7.45 us
  Pallas kernels: 0 us -> 33.1 us
  between operations: 16.2 us -> 0.05 us
  local copies, waits for them, and re-layouts: 14.8 us -> 1.36 us
  starting transfers between devices: 0.05 us -> 9.68 us
  blocking collectives: 8.23 us -> 0 us
    dot_general x3 -> x0, matrix products: 114 us -> none  [the longest x1 84.2 us: shards(): jnp.dot(inner_rows, fitted_rows, precision=precise, preferred_element_typ...]
    unnamed x4 -> x0, waiting for transfers between devices: 42.9 us -> none
    pallas_call x0 -> x2, Pallas kernels: none -> 33.1 us  [the longest x1 25.4 us: ladder_slots(): pl.pallas_call(ladder_kernel, out_shape=(out, out), in_specs=[pl.BlockSpe...]
    ppermute x0 -> x7, starting transfers between devices: none -> 9.68 us  [swap(): return lax.ppermute(x, axis, [(n, n ^ bit) for n in range(size)])]
    transpose x1 -> x0, local copies, waits for them, and re-layouts: 8.69 us -> none  [shards(): jnp.einsum('pac,ijdc->aijpd', window_factor, amplitude, precision=precise)]
    unnamed x1 -> x0, blocking collectives: 8.23 us -> none
    ppermute x0 -> x7, waiting for transfers between devices: none -> 7.45 us  [swap(): return lax.ppermute(x, axis, [(n, n ^ bit) for n in range(size)])]
    unnamed x12 -> x2, local copies, waits for them, and re-layouts: 6.07 us -> 1.34 us
  transfers between devices with their start and end apart: 2 -> 7, of which waited for: 2 -> 4; matrix products, arithmetic and copies ran while one was open for 7% -> 0% of each run, Pallas kernels for 0% -> 62%
where the time goes in v2:
time: 53.3 us; the launch traced here: 53.1 us
  Pallas kernels  33.1 us (62%)
  starting transfers between devices  9.68 us (18%)
  waiting for transfers between devices  7.45 us (14%)
  other arithmetic  1.49 us (3%)
  local copies, waits for them, and re-layouts  1.36 us (3%)
    pallas_call x1, Pallas kernels, ladder_slots(): pl.pallas_call(ladder_kernel, out_shape=(out, out), in_specs=[pl.BlockSpe...  25.4 us
    ppermute x7, starting transfers between devices, swap(): return lax.ppermute(x, axis, [(n, n ^ bit) for n in range(size)])  9.68 us
    pallas_call x1, Pallas kernels, cycle_slots(): pl.pallas_call(cycle_kernel, out_shape=(near, far, far), in_specs=[pl.Blo...  7.62 us
    ppermute x7, waiting for transfers between devices, swap(): return lax.ppermute(x, axis, [(n, n ^ bit) for n in range(size)])  7.45 us
    unnamed x2, local copies, waits for them, and re-layouts  1.34 us
  transfers between devices with their start and end apart: 7, of which 4 were waited for; matrix products, arithmetic and copies ran while one was open for 0% of the time, Pallas kernels for 62%

profile of v2, /device:TPU:0, one launch (start us, length us, event | category | flops | bytes accessed | tf_op | source)
XLA Modules:
  0.0 53.1 jit_solution(15497320585016703681)
XLA Ops:
  0.0 0.5 collective-permute-start
  0.5 7.6 %shard_map.55 = (f32[4,2,1024]{2,1,0:T(2,128)}, f32[2,2,1024]{2,1,0:T(2,128)}, f32[2,2,1024]{2,1,0:T(2,128)}) custom-call(f32[16,4096]{1,0:T(8,128)} %amps_hbm.1, f32[4096,1024]{1,0:T(8,128)} %panel_ref.1), custom_call_target="tpu_custom_call" | custom-call | flops 402653184 | bytes 16777216 | tf_op jit(solution)/shard_map/pallas_call | solution.py:87
  8.1 2.6 %collective-permute-start.1 = (f32[2,2,1024]{2,1,0:T(2,128)}, f32[2,2,1024]{2,1,0:T(2,128)S(1)}, u32[]{:S(2)}, u32[]{:S(2)}) collective-permute-start(f32[2,2,1024]{2,1,0:T(2,128)} %get-tuple-element.29), channel_id=1, source_target_pairs={{0,16},{8,24},{16,0},{24,8},{1,17},{9,25},{17,1},{25,9},{2,18},{10... | collective-permute-start | bytes 49160 | tf_op jit(solution)/shard_map/ppermute | solution.py:245
  10.6 0.2 collective-permute-start.2
  10.8 0.0 collective-permute-done.other_hbm
  10.8 0.0 copy-start
  10.8 1.3 %copy-done = f32[512,2,512]{2,1,0:T(2,128)} copy-done((f32[512,2,512]{2,1,0:T(2,128)}, f32[512,2,512]{2,1,0:T(2,128)S(1)}, u32[]{:S(2)}) %copy-start) | copy-done | bytes 2097176
  12.2 25.4 %shard_map.56 = (f32[2,8,1024]{2,1,0:T(8,128)}, f32[2,8,1024]{2,1,0:T(8,128)}) custom-call(f32[512,2,512]{2,1,0:T(2,128)} %own_hbm.1, f32[512,2,512]{2,1,0:T(2,128)} %copy-done, f32[16,128,512]{2,1,0:T(8,128)} %amp_hbm.1, f32[512,128,512]{2,1,0:T(8,128)} %fitted_hbm.1, f32[4,2,1024]{2,1,0:T(2,128)} %get-tuple-element.26.near_ref), custom_call_target="tpu_custom_call" | custom-call | flops 12884901888 | bytes 67108864 | tf_op jit(solution)/shard_map/pallas_call | solution.py:212
  37.6 0.0 collective-permute-done.1
  37.6 0.0 collective-permute-done.2
  37.6 0.1 collective-permute-start.3
  37.7 1.4 %collective-permute-done.3 = f32[2,8,1024]{2,1,0:T(8,128)S(1)} collective-permute-done((f32[2,8,1024]{2,1,0:T(8,128)}, f32[2,8,1024]{2,1,0:T(8,128)S(1)}, u32[]{:S(2)}, u32[]{:S(2)}) %collective-permute-start.3) | collective-permute-done | bytes 65568 | tf_op jit(solution)/shard_map/ppermute | solution.py:245
  39.2 0.9 %add.22 = f32[2,8,1024]{2,1,0:T(8,128)S(1)} add(f32[2,8,1024]{2,1,0:T(8,128)} %get-tuple-element.31, f32[2,8,1024]{2,1,0:T(8,128)S(1)} %collective-permute-done.3) | non-fusion elementwise | flops 16384 | bytes 196608 | tf_op jit(solution)/shard_map/add | solution.py:254
  40.1 1.8 %collective-permute-start.4 = (f32[8,1024]{1,0:T(8,128)S(1)}, f32[8,1024]{1,0:T(8,128)S(1)}, u32[]{:S(2)}, u32[]{:S(2)}) collective-permute-start(f32[8,1024]{1,0:T(8,128)S(1)} %slice_bitcast_fusion), channel_id=1, source_target_pairs={{0,4},{4,0},{1,5},{5,1},{2,6},{6,2},{3,7},{7,3},{8,12},{12,8},{9,1... | collective-permute-start | bytes 98312 | tf_op jit(solution)/shard_map/ppermute | solution.py:245
  41.8 2.2 %collective-permute-done.4 = f32[8,1024]{1,0:T(8,128)S(1)} collective-permute-done((f32[8,1024]{1,0:T(8,128)S(1)}, f32[8,1024]{1,0:T(8,128)S(1)}, u32[]{:S(2)}, u32[]{:S(2)}) %collective-permute-start.4) | collective-permute-done | bytes 32800 | tf_op jit(solution)/shard_map/ppermute | solution.py:245
  44.0 2.8 %collective-permute-start.5 = (f32[4,1024]{1,0:T(4,128)S(1)}, f32[4,1024]{1,0:T(4,128)S(1)}, u32[]{:S(2)}, u32[]{:S(2)}) collective-permute-start(f32[4,1024]{1,0:T(4,128)S(1)} %slice.53), channel_id=1, source_target_pairs={{0,2},{1,3},{2,0},{3,1},{4,6},{5,7},{6,4},{7,5},{8,10},{9,11},{10,... | collective-permute-start | bytes 49160 | tf_op jit(solution)/shard_map/ppermute | solution.py:245
  46.9 1.9 %collective-permute-done.5 = f32[4,1024]{1,0:T(4,128)S(1)} collective-permute-done((f32[4,1024]{1,0:T(4,128)S(1)}, f32[4,1024]{1,0:T(4,128)S(1)}, u32[]{:S(2)}, u32[]{:S(2)}) %collective-permute-start.5) | collective-permute-done | bytes 16416 | tf_op jit(solution)/shard_map/ppermute | solution.py:245
  48.8 1.8 %collective-permute-start.6 = (f32[2,1024]{1,0:T(2,128)S(1)}, f32[2,1024]{1,0:T(2,128)S(1)}, u32[]{:S(2)}, u32[]{:S(2)}) collective-permute-start(f32[2,1024]{1,0:T(2,128)S(1)} %slice.55), channel_id=1, source_target_pairs={{0,1},{1,0},{2,3},{3,2},{4,5},{5,4},{6,7},{7,6},{8,9},{9,8},{10,11... | collective-permute-start | bytes 24584 | tf_op jit(solution)/shard_map/ppermute | solution.py:245
  50.6 1.9 %collective-permute-done.6 = f32[2,1024]{1,0:T(2,128)S(1)} collective-permute-done((f32[2,1024]{1,0:T(2,128)S(1)}, f32[2,1024]{1,0:T(2,128)S(1)}, u32[]{:S(2)}, u32[]{:S(2)}) %collective-permute-start.6) | collective-permute-done | bytes 8224 | tf_op jit(solution)/shard_map/ppermute | solution.py:245
  52.5 0.6 %slice_add_fusion.2 = f32[2,1024]{1,0:T(2,128)} fusion(f32[2,1024]{1,0:T(2,128)S(1)} %collective-permute-done.6, f32[4,1024]{1,0:T(4,128)S(1)} %slice_add_fusion), kind=kLoop, calls=%fused_computation.6 | loop fusion | flops 2048 | bytes 24576 | tf_op jit(solution)/shard_map/add | solution.py:258
  (6 shorter events, 0.1 us)
Async XLA Ops:
  0.0 10.8 %collective-permute-start = (f32[512,2,512]{2,1,0:T(2,128)}, f32[512,2,512]{2,1,0:T(2,128)S(1)}, u32[]{:S(2)}, u32[]{:S(2)}) collective-permute-start(f32[512,2,512]{2,1,0:T(2,128)} %own_hbm.1), channel_id=1, source_target_pairs={{0,8},{8,0},{16,24},{24,16},{1,9},{9,1},{17,25},{25,17},{2,10},{10... | collective-permute-start | bytes 6291464 | tf_op jit(solution)/shard_map/ppermute | solution.py:245
  8.1 29.5 %collective-permute-start.1 = (f32[2,2,1024]{2,1,0:T(2,128)}, f32[2,2,1024]{2,1,0:T(2,128)S(1)}, u32[]{:S(2)}, u32[]{:S(2)}) collective-permute-start(f32[2,2,1024]{2,1,0:T(2,128)} %get-tuple-element.29), channel_id=1, source_target_pairs={{0,16},{8,24},{16,0},{24,8},{1,17},{9,25},{17,1},{25,9},{2,18},{10... | collective-permute-start | bytes 49160 | tf_op jit(solution)/shard_map/ppermute | solution.py:245
  10.6 27.0 %collective-permute-start.2 = (f32[2,2,1024]{2,1,0:T(2,128)}, f32[2,2,1024]{2,1,0:T(2,128)S(1)}, u32[]{:S(2)}, u32[]{:S(2)}) collective-permute-start(f32[2,2,1024]{2,1,0:T(2,128)} %get-tuple-element.30), channel_id=1, source_target_pairs={{0,24},{8,16},{16,8},{24,0},{1,25},{9,17},{17,9},{25,1},{2,26},{10... | collective-permute-start | bytes 49160 | tf_op jit(solution)/shard_map/ppermute | solution.py:245
  10.8 1.3 %copy-start = (f32[512,2,512]{2,1,0:T(2,128)}, f32[512,2,512]{2,1,0:T(2,128)S(1)}, u32[]{:S(2)}) copy-start(f32[512,2,512]{2,1,0:T(2,128)S(1)} %collective-permute-done.other_hbm) | copy-start | bytes 6291460
  37.6 1.5 %collective-permute-start.3 = (f32[2,8,1024]{2,1,0:T(8,128)}, f32[2,8,1024]{2,1,0:T(8,128)S(1)}, u32[]{:S(2)}, u32[]{:S(2)}) collective-permute-start(f32[2,8,1024]{2,1,0:T(8,128)} %get-tuple-element.32), channel_id=1, source_target_pairs={{0,8},{8,0},{16,24},{24,16},{1,9},{9,1},{17,25},{25,17},{2,10},{10... | collective-permute-start | bytes 196616 | tf_op jit(solution)/shard_map/ppermute | solution.py:245
  40.1 4.0 %collective-permute-start.4 = (f32[8,1024]{1,0:T(8,128)S(1)}, f32[8,1024]{1,0:T(8,128)S(1)}, u32[]{:S(2)}, u32[]{:S(2)}) collective-permute-start(f32[8,1024]{1,0:T(8,128)S(1)} %slice_bitcast_fusion), channel_id=1, source_target_pairs={{0,4},{4,0},{1,5},{5,1},{2,6},{6,2},{3,7},{7,3},{8,12},{12,8},{9,1... | collective-permute-start | bytes 98312 | tf_op jit(solution)/shard_map/ppermute | solution.py:245
  44.0 4.7 %collective-permute-start.5 = (f32[4,1024]{1,0:T(4,128)S(1)}, f32[4,1024]{1,0:T(4,128)S(1)}, u32[]{:S(2)}, u32[]{:S(2)}) collective-permute-start(f32[4,1024]{1,0:T(4,128)S(1)} %slice.53), channel_id=1, source_target_pairs={{0,2},{1,3},{2,0},{3,1},{4,6},{5,7},{6,4},{7,5},{8,10},{9,11},{10,... | collective-permute-start | bytes 49160 | tf_op jit(solution)/shard_map/ppermute | solution.py:245
  48.8 3.7 %collective-permute-start.6 = (f32[2,1024]{1,0:T(2,128)S(1)}, f32[2,1024]{1,0:T(2,128)S(1)}, u32[]{:S(2)}, u32[]{:S(2)}) collective-permute-start(f32[2,1024]{1,0:T(2,128)S(1)} %slice.55), channel_id=1, source_target_pairs={{0,1},{1,0},{2,3},{3,2},{4,5},{5,4},{6,7},{7,6},{8,9},{9,8},{10,11... | collective-permute-start | bytes 24584 | tf_op jit(solution)/shard_map/ppermute | solution.py:245

commit v3 on v2

--- a/solution.py
+++ b/solution.py
@@ -9,7 +9,7 @@
 
 NI = 2
 NJ = 8
-VMEM_BYTES = 56 * 1024 * 1024
+VMEM_BYTES = 48 * 1024 * 1024
 LANES = 128
 
 
@@ -109,8 +109,8 @@
 PART = 2
 
 
-def ladder_kernel(own_hbm, other_hbm, amp_hbm, fitted_hbm, near_ref, keep_ref, send_ref,
-                  own, other, amp, amp_high, amp_low, rows_ref, left, fitted_in, total, sems, fitted_sems):
+def ladder_kernel(own_hbm, other, amp_hbm, fitted_hbm, near_ref, keep_ref, send_ref,
+                  own, amp, amp_high, amp_low, rows_ref, left, fitted_in, total, sems, fitted_sems):
     pairs, fit_count, virtuals = amp_hbm.shape
     aux_half, a_count = own.shape[:2]
     steps = aux_half // DEPTH
@@ -125,7 +125,6 @@
     small = [
         pltpu.make_async_copy(amp_hbm, amp, sems.at[0]),
         pltpu.make_async_copy(own_hbm.at[pl.ds(first, aux_half)], own, sems.at[1]),
-        pltpu.make_async_copy(other_hbm.at[pl.ds(first, aux_half)], other, sems.at[2]),
     ]
     for copy in small:
         copy.start()
@@ -138,7 +137,6 @@
         amp_high[pl.ds(pair * fit_count, fit_count), :] = high
         amp_low[pl.ds(pair * fit_count, fit_count), :] = low
     small[1].wait()
-    small[2].wait()
     for step in range(2, SLOTS):
         fetch(step, step).start()
 
@@ -146,7 +144,7 @@
         count = DEPTH * GROUP
         for p in range(count):
             rows_ref[pl.ds(2 * a_count * p, a_count), :] = own[group * count + p]
-            rows_ref[pl.ds(2 * a_count * p + a_count, a_count), :] = other[group * count + p]
+            rows_ref[pl.ds(2 * a_count * p + a_count, a_count), :] = other[first + group * count + p]
         high, low = split(rows_ref[...])
         stacked = jnp.concatenate([high, low], axis=0)
         n_rows = high.shape[0]
@@ -214,14 +212,13 @@
         out_shape=(out, out),
         in_specs=[
             pl.BlockSpec(memory_space=pltpu.HBM),
-            pl.BlockSpec(memory_space=pl.ANY),
+            pl.BlockSpec(memory_space=pltpu.VMEM),
             pl.BlockSpec(memory_space=pltpu.HBM),
             pl.BlockSpec(memory_space=pltpu.HBM),
             pl.BlockSpec(memory_space=pltpu.VMEM),
         ],
         out_specs=(pl.BlockSpec(memory_space=pltpu.VMEM),) * 2,
         scratch_shapes=[
-            pltpu.VMEM(half, jnp.float32),
             pltpu.VMEM(half, jnp.float32),
             pltpu.VMEM(pair_amps.shape, jnp.float32),
             pltpu.VMEM((pairs * fit_count, virtuals), jnp.bfloat16),
@@ -230,7 +227,7 @@
             pltpu.VMEM((GROUP, 2 * m, DEPTH * LANES), jnp.bfloat16),
             pltpu.VMEM((SLOTS, DEPTH, fit_count, virtuals), jnp.float32),
             pltpu.VMEM((m, virtuals), jnp.float32),
-            pltpu.SemaphoreType.DMA((3,)),
+            pltpu.SemaphoreType.DMA((2,)),
             pltpu.SemaphoreType.DMA((SLOTS,)),
         ],
         compiler_params=pltpu.CompilerParams(vmem_limit_bytes=VMEM_BYTES),

time: 53.3 us -> 48.8 us (0.916)
  Pallas kernels: 33.1 us -> 30 us
  other arithmetic: 1.49 us -> 0.65 us
  waiting for transfers between devices: 7.45 us -> 6.86 us
    pallas_call x1, Pallas kernels: 25.4 us -> 23.4 us  [ladder_slots(): pl.pallas_call(ladder_kernel, out_shape=(out, out), in_specs=[pl.BlockSpe...]
    pallas_call x1, Pallas kernels: 7.62 us -> 6.69 us  [cycle_slots(): pl.pallas_call(cycle_kernel, out_shape=(near, far, far), in_specs=[pl.Blo...]
    add x1, other arithmetic: 0.85 us -> 0.01 us  [fast(): total = (keep + swap(send, 'grp', grp_count, 1)).at[:, :NI].add(one + two)]
    ppermute x7, waiting for transfers between devices: 7.45 us -> 6.86 us  [swap(): return lax.ppermute(x, axis, [(n, n ^ bit) for n in range(size)])]
    unnamed x2 -> x4, local copies, waits for them, and re-layouts: 1.34 us -> 1.13 us
where the time goes in v3:
time: 48.8 us; the launch traced here: 48.6 us
  Pallas kernels  30 us (61%)
  starting transfers between devices  9.89 us (20%)
  waiting for transfers between devices  6.86 us (14%)
  local copies, waits for them, and re-layouts  1.15 us (2%)
  other arithmetic  0.65 us (1%)
    pallas_call x1, Pallas kernels, ladder_slots(): pl.pallas_call(ladder_kernel, out_shape=(out, out), in_specs=[pl.BlockSpe...  23.4 us
    ppermute x7, starting transfers between devices, swap(): return lax.ppermute(x, axis, [(n, n ^ bit) for n in range(size)])  9.89 us
    ppermute x7, waiting for transfers between devices, swap(): return lax.ppermute(x, axis, [(n, n ^ bit) for n in range(size)])  6.86 us
    pallas_call x1, Pallas kernels, cycle_slots(): pl.pallas_call(cycle_kernel, out_shape=(near, far, far), in_specs=[pl.Blo...  6.69 us
    unnamed x4, local copies, waits for them, and re-layouts  1.13 us
  transfers between devices with their start and end apart: 7, of which 4 were waited for; matrix products, arithmetic and copies ran while one was open for 0% of the time, Pallas kernels for 62%

profile of v3, /device:TPU:0, one launch (start us, length us, event | category | flops | bytes accessed | tf_op | source)
XLA Modules:
  0.0 48.6 jit_solution(14691562202969752575)
XLA Ops:
  0.0 0.0 copy-start
  0.0 0.5 collective-permute-start
  0.5 0.0 copy-start.1
  0.5 1.1 %copy-done.1 = f32[16,4096]{1,0:T(8,128)S(1)} copy-done((f32[16,4096]{1,0:T(8,128)S(1)}, f32[16,4096]{1,0:T(8,128)}, u32[]{:S(2)}) %copy-start.1) | copy-done | bytes 262168
  1.6 6.7 %shard_map.55 = (f32[4,2,1024]{2,1,0:T(2,128)S(1)}, f32[2,2,1024]{2,1,0:T(2,128)S(1)}, f32[2,2,1024]{2,1,0:T(2,128)S(1)}) custom-call(f32[16,4096]{1,0:T(8,128)S(1)} %copy-done.1, f32[4096,1024]{1,0:T(8,128)} %panel_ref.1), custom_call_target="tpu_custom_call" | custom-call | flops 402653184 | bytes 16777216 | tf_op jit(solution)/shard_map/pallas_call | solution.py:87
  8.3 2.5 %collective-permute-start.1 = (f32[2,2,1024]{2,1,0:T(2,128)S(1)}, f32[2,2,1024]{2,1,0:T(2,128)S(1)}, u32[]{:S(2)}, u32[]{:S(2)}) collective-permute-start(f32[2,2,1024]{2,1,0:T(2,128)S(1)} %get-tuple-element.29), channel_id=1, source_target_pairs={{0,16},{8,24},{16,0},{24,8},{1,17},{9,25},{17,1},{25,9},{2,18},{10... | collective-permute-start | bytes 49160 | tf_op jit(solution)/shard_map/ppermute | solution.py:242
  10.8 0.0 collective-permute-start.2
  10.8 0.0 collective-permute-done.other
  10.8 0.0 copy-done
  10.9 23.4 %shard_map.56 = (f32[2,8,1024]{2,1,0:T(8,128)S(1)}, f32[2,8,1024]{2,1,0:T(8,128)S(1)}) custom-call(f32[512,2,512]{2,1,0:T(2,128)S(1)} %copy-done, f32[512,2,512]{2,1,0:T(2,128)S(1)} %collective-permute-done.other, f32[16,128,512]{2,1,0:T(8,128)} %amp_hbm.1, f32[512,128,512]{2,1,0:T(8,128)} %fitted_hbm.1, f32[4,2,1024]{2,1,0:T(2,128)S(1)} %get-tuple-element.26.near_ref), custom_call_target="tpu_custom_call" | custom-call | flops 12884901888 | bytes 67108864 | tf_op jit(solution)/shard_map/pallas_call | solution.py:210
  34.2 0.0 collective-permute-done.1
  34.2 0.0 collective-permute-done.2
  34.2 0.2 collective-permute-start.3
  34.5 1.1 %collective-permute-done.3 = f32[2,8,1024]{2,1,0:T(8,128)S(1)} collective-permute-done((f32[2,8,1024]{2,1,0:T(8,128)S(1)}, f32[2,8,1024]{2,1,0:T(8,128)S(1)}, u32[]{:S(2)}, u32[]{:S(2)}) %collective-permute-start.3) | collective-permute-done | bytes 65568 | tf_op jit(solution)/shard_map/ppermute | solution.py:242
  35.6 1.8 %collective-permute-start.4 = (f32[8,1024]{1,0:T(8,128)S(1)}, f32[8,1024]{1,0:T(8,128)S(1)}, u32[]{:S(2)}, u32[]{:S(2)}) collective-permute-start(f32[8,1024]{1,0:T(8,128)S(1)} %slice_bitcast_fusion), channel_id=1, source_target_pairs={{0,4},{4,0},{1,5},{5,1},{2,6},{6,2},{3,7},{7,3},{8,12},{12,8},{9,1... | collective-permute-start | bytes 98312 | tf_op jit(solution)/shard_map/ppermute | solution.py:242
  37.4 2.2 %collective-permute-done.4 = f32[8,1024]{1,0:T(8,128)S(1)} collective-permute-done((f32[8,1024]{1,0:T(8,128)S(1)}, f32[8,1024]{1,0:T(8,128)S(1)}, u32[]{:S(2)}, u32[]{:S(2)}) %collective-permute-start.4) | collective-permute-done | bytes 32800 | tf_op jit(solution)/shard_map/ppermute | solution.py:242
  39.6 2.9 %collective-permute-start.5 = (f32[4,1024]{1,0:T(4,128)S(1)}, f32[4,1024]{1,0:T(4,128)S(1)}, u32[]{:S(2)}, u32[]{:S(2)}) collective-permute-start(f32[4,1024]{1,0:T(4,128)S(1)} %slice.53), channel_id=1, source_target_pairs={{0,2},{1,3},{2,0},{3,1},{4,6},{5,7},{6,4},{7,5},{8,10},{9,11},{10,... | collective-permute-start | bytes 49160 | tf_op jit(solution)/shard_map/ppermute | solution.py:242
  42.5 1.8 %collective-permute-done.5 = f32[4,1024]{1,0:T(4,128)S(1)} collective-permute-done((f32[4,1024]{1,0:T(4,128)S(1)}, f32[4,1024]{1,0:T(4,128)S(1)}, u32[]{:S(2)}, u32[]{:S(2)}) %collective-permute-start.5) | collective-permute-done | bytes 16416 | tf_op jit(solution)/shard_map/ppermute | solution.py:242
  44.3 1.9 %collective-permute-start.6 = (f32[2,1024]{1,0:T(2,128)S(1)}, f32[2,1024]{1,0:T(2,128)S(1)}, u32[]{:S(2)}, u32[]{:S(2)}) collective-permute-start(f32[2,1024]{1,0:T(2,128)S(1)} %slice.55), channel_id=1, source_target_pairs={{0,1},{1,0},{2,3},{3,2},{4,5},{5,4},{6,7},{7,6},{8,9},{9,8},{10,11... | collective-permute-start | bytes 24584 | tf_op jit(solution)/shard_map/ppermute | solution.py:242
  46.2 1.8 %collective-permute-done.6 = f32[2,1024]{1,0:T(2,128)S(1)} collective-permute-done((f32[2,1024]{1,0:T(2,128)S(1)}, f32[2,1024]{1,0:T(2,128)S(1)}, u32[]{:S(2)}, u32[]{:S(2)}) %collective-permute-start.6) | collective-permute-done | bytes 8224 | tf_op jit(solution)/shard_map/ppermute | solution.py:242
  48.0 0.6 %slice_add_fusion.2 = f32[2,1024]{1,0:T(2,128)} fusion(f32[2,1024]{1,0:T(2,128)S(1)} %collective-permute-done.6, f32[4,1024]{1,0:T(4,128)S(1)} %slice_add_fusion), kind=kLoop, calls=%fused_computation.6 | loop fusion | flops 2048 | bytes 24576 | tf_op jit(solution)/shard_map/add | solution.py:255
  (7 shorter events, 0.1 us)
Async XLA Ops:
  0.0 10.9 %copy-start = (f32[512,2,512]{2,1,0:T(2,128)S(1)}, f32[512,2,512]{2,1,0:T(2,128)}, u32[]{:S(2)}) copy-start(f32[512,2,512]{2,1,0:T(2,128)} %own_hbm.1) | copy-start | bytes 6291460
  0.0 10.8 %collective-permute-start = (f32[512,2,512]{2,1,0:T(2,128)}, f32[512,2,512]{2,1,0:T(2,128)S(1)}, u32[]{:S(2)}, u32[]{:S(2)}) collective-permute-start(f32[512,2,512]{2,1,0:T(2,128)} %own_hbm.1), channel_id=1, source_target_pairs={{0,8},{8,0},{16,24},{24,16},{1,9},{9,1},{17,25},{25,17},{2,10},{10... | collective-permute-start | bytes 6291464 | tf_op jit(solution)/shard_map/ppermute | solution.py:242
  0.5 1.1 %copy-start.1 = (f32[16,4096]{1,0:T(8,128)S(1)}, f32[16,4096]{1,0:T(8,128)}, u32[]{:S(2)}) copy-start(f32[16,4096]{1,0:T(8,128)} %amps_hbm.1) | copy-start | bytes 786436
  8.3 25.9 %collective-permute-start.1 = (f32[2,2,1024]{2,1,0:T(2,128)S(1)}, f32[2,2,1024]{2,1,0:T(2,128)S(1)}, u32[]{:S(2)}, u32[]{:S(2)}) collective-permute-start(f32[2,2,1024]{2,1,0:T(2,128)S(1)} %get-tuple-element.29), channel_id=1, source_target_pairs={{0,16},{8,24},{16,0},{24,8},{1,17},{9,25},{17,1},{25,9},{2,18},{10... | collective-permute-start | bytes 49160 | tf_op jit(solution)/shard_map/ppermute | solution.py:242
  10.8 23.4 %collective-permute-start.2 = (f32[2,2,1024]{2,1,0:T(2,128)S(1)}, f32[2,2,1024]{2,1,0:T(2,128)S(1)}, u32[]{:S(2)}, u32[]{:S(2)}) collective-permute-start(f32[2,2,1024]{2,1,0:T(2,128)S(1)} %get-tuple-element.30), channel_id=1, source_target_pairs={{0,24},{8,16},{16,8},{24,0},{1,25},{9,17},{17,9},{25,1},{2,26},{10... | collective-permute-start | bytes 49160 | tf_op jit(solution)/shard_map/ppermute | solution.py:242
  34.2 1.3 %collective-permute-start.3 = (f32[2,8,1024]{2,1,0:T(8,128)S(1)}, f32[2,8,1024]{2,1,0:T(8,128)S(1)}, u32[]{:S(2)}, u32[]{:S(2)}) collective-permute-start(f32[2,8,1024]{2,1,0:T(8,128)S(1)} %get-tuple-element.32), channel_id=1, source_target_pairs={{0,8},{8,0},{16,24},{24,16},{1,9},{9,1},{17,25},{25,17},{2,10},{10... | collective-permute-start | bytes 196616 | tf_op jit(solution)/shard_map/ppermute | solution.py:242
  35.6 4.0 %collective-permute-start.4 = (f32[8,1024]{1,0:T(8,128)S(1)}, f32[8,1024]{1,0:T(8,128)S(1)}, u32[]{:S(2)}, u32[]{:S(2)}) collective-permute-start(f32[8,1024]{1,0:T(8,128)S(1)} %slice_bitcast_fusion), channel_id=1, source_target_pairs={{0,4},{4,0},{1,5},{5,1},{2,6},{6,2},{3,7},{7,3},{8,12},{12,8},{9,1... | collective-permute-start | bytes 98312 | tf_op jit(solution)/shard_map/ppermute | solution.py:242
  39.6 4.7 %collective-permute-start.5 = (f32[4,1024]{1,0:T(4,128)S(1)}, f32[4,1024]{1,0:T(4,128)S(1)}, u32[]{:S(2)}, u32[]{:S(2)}) collective-permute-start(f32[4,1024]{1,0:T(4,128)S(1)} %slice.53), channel_id=1, source_target_pairs={{0,2},{1,3},{2,0},{3,1},{4,6},{5,7},{6,4},{7,5},{8,10},{9,11},{10,... | collective-permute-start | bytes 49160 | tf_op jit(solution)/shard_map/ppermute | solution.py:242
  44.3 3.7 %collective-permute-start.6 = (f32[2,1024]{1,0:T(2,128)S(1)}, f32[2,1024]{1,0:T(2,128)S(1)}, u32[]{:S(2)}, u32[]{:S(2)}) collective-permute-start(f32[2,1024]{1,0:T(2,128)S(1)} %slice.55), channel_id=1, source_target_pairs={{0,1},{1,0},{2,3},{3,2},{4,5},{5,4},{6,7},{7,6},{8,9},{9,8},{10,11... | collective-permute-start | bytes 24584 | tf_op jit(solution)/shard_map/ppermute | solution.py:242

commit v4 on v3

--- a/solution.py
+++ b/solution.py
@@ -9,7 +9,7 @@
 
 NI = 2
 NJ = 8
-VMEM_BYTES = 48 * 1024 * 1024
+VMEM_BYTES = 38 * 1024 * 1024
 LANES = 128
 
 
@@ -109,10 +109,10 @@
 PART = 2
 
 
-def ladder_kernel(own_hbm, other, amp_hbm, fitted_hbm, near_ref, keep_ref, send_ref,
-                  own, amp, amp_high, amp_low, rows_ref, left, fitted_in, total, sems, fitted_sems):
-    pairs, fit_count, virtuals = amp_hbm.shape
-    aux_half, a_count = own.shape[:2]
+def ladder_kernel(own, other, amp, fitted_hbm, near_ref, keep_ref, send_ref,
+                  amp_high, amp_low, rows_ref, left, fitted_in, total, fitted_sems):
+    pairs, fit_count, virtuals = amp.shape
+    aux_half, a_count = own.shape[0] // 2, own.shape[1]
     steps = aux_half // DEPTH
     core, exc, col = lax.axis_index("grp") % 2, lax.axis_index("exc"), lax.axis_index("col")
     first = core * aux_half
@@ -122,28 +122,20 @@
         source = fitted_hbm.at[pl.ds(first + step * DEPTH, DEPTH)]
         return pltpu.make_async_copy(source, fitted_in.at[slot], fitted_sems.at[slot])
 
-    small = [
-        pltpu.make_async_copy(amp_hbm, amp, sems.at[0]),
-        pltpu.make_async_copy(own_hbm.at[pl.ds(first, aux_half)], own, sems.at[1]),
-    ]
-    for copy in small:
-        copy.start()
     fetch(0, 0).start()
     total[...] = jnp.zeros_like(total)
-    small[0].wait()
     fetch(1, 1).start()
     for pair in range(pairs):
         high, low = split(amp[pair])
         amp_high[pl.ds(pair * fit_count, fit_count), :] = high
         amp_low[pl.ds(pair * fit_count, fit_count), :] = low
-    small[1].wait()
     for step in range(2, SLOTS):
         fetch(step, step).start()
 
     def first_product(group):
         count = DEPTH * GROUP
         for p in range(count):
-            rows_ref[pl.ds(2 * a_count * p, a_count), :] = own[group * count + p]
+            rows_ref[pl.ds(2 * a_count * p, a_count), :] = own[first + group * count + p]
             rows_ref[pl.ds(2 * a_count * p + a_count, a_count), :] = other[first + group * count + p]
         high, low = split(rows_ref[...])
         stacked = jnp.concatenate([high, low], axis=0)
@@ -206,28 +198,24 @@
     aux_count, a_count = own.shape[:2]
     m = 2 * a_count * pairs
     out = jax.ShapeDtypeStruct((2, NJ, 2 * virtuals), jnp.float32)
-    half = (aux_count // 2, a_count, virtuals)
     return pl.pallas_call(
         ladder_kernel,
         out_shape=(out, out),
         in_specs=[
-            pl.BlockSpec(memory_space=pltpu.HBM),
-            pl.BlockSpec(memory_space=pltpu.VMEM),
-            pl.BlockSpec(memory_space=pltpu.HBM),
+            pl.BlockSpec(memory_space=pltpu.VMEM),
+            pl.BlockSpec(memory_space=pltpu.VMEM),
+            pl.BlockSpec(memory_space=pltpu.VMEM),
             pl.BlockSpec(memory_space=pltpu.HBM),
             pl.BlockSpec(memory_space=pltpu.VMEM),
         ],
         out_specs=(pl.BlockSpec(memory_space=pltpu.VMEM),) * 2,
         scratch_shapes=[
-            pltpu.VMEM(half, jnp.float32),
-            pltpu.VMEM(pair_amps.shape, jnp.float32),
             pltpu.VMEM((pairs * fit_count, virtuals), jnp.bfloat16),
             pltpu.VMEM((pairs * fit_count, virtuals), jnp.bfloat16),
             pltpu.VMEM((DEPTH * GROUP * 2 * a_count, virtuals), jnp.float32),
             pltpu.VMEM((GROUP, 2 * m, DEPTH * LANES), jnp.bfloat16),
             pltpu.VMEM((SLOTS, DEPTH, fit_count, virtuals), jnp.float32),
             pltpu.VMEM((m, virtuals), jnp.float32),
-            pltpu.SemaphoreType.DMA((2,)),
             pltpu.SemaphoreType.DMA((SLOTS,)),
         ],
         compiler_params=pltpu.CompilerParams(vmem_limit_bytes=VMEM_BYTES),

time: 48.8 us -> 48 us (0.984)
  Pallas kernels: 30 us -> 28.9 us
  starting transfers between devices: 9.89 us -> 10.4 us
    pallas_call x1, Pallas kernels: 23.4 us -> 22 us  [ladder_slots(): pl.pallas_call(ladder_kernel, out_shape=(out, out), in_specs=[pl.BlockSpe...]
    unnamed x4 -> x6, local copies, waits for them, and re-layouts: 1.13 us -> 1.18 us
  transfers between devices with their start and end apart: 7 -> 7, of which waited for: 4 -> 4; matrix products, arithmetic and copies ran while one was open for 0% -> 0% of each run, Pallas kernels for 62% -> 61%
where the time goes in v4:
time: 48 us; the launch traced here: 47.8 us
  Pallas kernels  28.9 us (60%)
  starting transfers between devices  10.4 us (22%)
  waiting for transfers between devices  6.63 us (14%)
  local copies, waits for them, and re-layouts  1.2 us (2%)
  other arithmetic  0.65 us (1%)
    pallas_call x1, Pallas kernels, ladder_slots(): pl.pallas_call(ladder_kernel, out_shape=(out, out), in_specs=[pl.BlockSpe...  22 us
    ppermute x7, starting transfers between devices, swap(): return lax.ppermute(x, axis, [(n, n ^ bit) for n in range(size)])  10.4 us
    pallas_call x1, Pallas kernels, cycle_slots(): pl.pallas_call(cycle_kernel, out_shape=(near, far, far), in_specs=[pl.Blo...  6.96 us
    ppermute x7, waiting for transfers between devices, swap(): return lax.ppermute(x, axis, [(n, n ^ bit) for n in range(size)])  6.63 us
    unnamed x6, local copies, waits for them, and re-layouts  1.18 us
  transfers between devices with their start and end apart: 7, of which 4 were waited for; matrix products, arithmetic and copies ran while one was open for 0% of the time, Pallas kernels for 61%

profile of v4, /device:TPU:0, one launch (start us, length us, event | category | flops | bytes accessed | tf_op | source)
XLA Modules:
  0.0 47.8 jit_solution(1693561203105270986)
XLA Ops:
  0.0 0.0 copy-start.1
  0.0 0.0 copy-start
  0.0 0.5 collective-permute-start
  0.5 0.0 copy-start.2
  0.5 1.2 %copy-done.2 = f32[16,4096]{1,0:T(8,128)S(1)} copy-done((f32[16,4096]{1,0:T(8,128)S(1)}, f32[16,4096]{1,0:T(8,128)}, u32[]{:S(2)}) %copy-start.2) | copy-done | bytes 262168
  1.6 7.0 %shard_map.55 = (f32[4,2,1024]{2,1,0:T(2,128)S(1)}, f32[2,2,1024]{2,1,0:T(2,128)S(1)}, f32[2,2,1024]{2,1,0:T(2,128)S(1)}) custom-call(f32[16,4096]{1,0:T(8,128)S(1)} %copy-done.2, f32[4096,1024]{1,0:T(8,128)} %panel_ref.1), custom_call_target="tpu_custom_call" | custom-call | flops 402653184 | bytes 16777216 | tf_op jit(solution)/shard_map/pallas_call | solution.py:87
  8.6 2.8 %collective-permute-start.1 = (f32[2,2,1024]{2,1,0:T(2,128)S(1)}, f32[2,2,1024]{2,1,0:T(2,128)S(1)}, u32[]{:S(2)}, u32[]{:S(2)}) collective-permute-start(f32[2,2,1024]{2,1,0:T(2,128)S(1)} %get-tuple-element.29), channel_id=1, source_target_pairs={{0,16},{8,24},{16,0},{24,8},{1,17},{9,25},{17,1},{25,9},{2,18},{10... | collective-permute-start | bytes 49160 | tf_op jit(solution)/shard_map/ppermute | solution.py:230
  11.4 0.0 collective-permute-start.2
  11.4 0.0 collective-permute-done.other
  11.4 0.0 copy-done.1
  11.4 0.0 copy-done
  11.4 22.0 %shard_map.56 = (f32[2,8,1024]{2,1,0:T(8,128)S(1)}, f32[2,8,1024]{2,1,0:T(8,128)S(1)}) custom-call(f32[512,2,512]{2,1,0:T(2,128)S(1)} %copy-done.1, f32[512,2,512]{2,1,0:T(2,128)S(1)} %collective-permute-done.other, f32[16,128,512]{2,1,0:T(8,128)S(1)} %copy-done, f32[512,128,512]{2,1,0:T(8,128)} %fitted_hbm.1, f32[4,2,1024]{2,1,0:T(2,128)S(1)} %get-tuple-element.26.near_ref), custom_call_target="tpu_custom_call" | custom-call | flops 12884901888 | bytes 67108864 | tf_op jit(solution)/shard_map/pallas_call | solution.py:201
  33.4 0.0 collective-permute-done.1
  33.4 0.0 collective-permute-done.2
  33.4 0.3 collective-permute-start.3
  33.7 1.0 %collective-permute-done.3 = f32[2,8,1024]{2,1,0:T(8,128)S(1)} collective-permute-done((f32[2,8,1024]{2,1,0:T(8,128)S(1)}, f32[2,8,1024]{2,1,0:T(8,128)S(1)}, u32[]{:S(2)}, u32[]{:S(2)}) %collective-permute-start.3) | collective-permute-done | bytes 65568 | tf_op jit(solution)/shard_map/ppermute | solution.py:230
  34.8 1.9 %collective-permute-start.4 = (f32[8,1024]{1,0:T(8,128)S(1)}, f32[8,1024]{1,0:T(8,128)S(1)}, u32[]{:S(2)}, u32[]{:S(2)}) collective-permute-start(f32[8,1024]{1,0:T(8,128)S(1)} %slice_bitcast_fusion), channel_id=1, source_target_pairs={{0,4},{4,0},{1,5},{5,1},{2,6},{6,2},{3,7},{7,3},{8,12},{12,8},{9,1... | collective-permute-start | bytes 98312 | tf_op jit(solution)/shard_map/ppermute | solution.py:230
  36.7 2.1 %collective-permute-done.4 = f32[8,1024]{1,0:T(8,128)S(1)} collective-permute-done((f32[8,1024]{1,0:T(8,128)S(1)}, f32[8,1024]{1,0:T(8,128)S(1)}, u32[]{:S(2)}, u32[]{:S(2)}) %collective-permute-start.4) | collective-permute-done | bytes 32800 | tf_op jit(solution)/shard_map/ppermute | solution.py:230
  38.8 3.0 %collective-permute-start.5 = (f32[4,1024]{1,0:T(4,128)S(1)}, f32[4,1024]{1,0:T(4,128)S(1)}, u32[]{:S(2)}, u32[]{:S(2)}) collective-permute-start(f32[4,1024]{1,0:T(4,128)S(1)} %slice.53), channel_id=1, source_target_pairs={{0,2},{1,3},{2,0},{3,1},{4,6},{5,7},{6,4},{7,5},{8,10},{9,11},{10,... | collective-permute-start | bytes 49160 | tf_op jit(solution)/shard_map/ppermute | solution.py:230
  41.8 1.7 %collective-permute-done.5 = f32[4,1024]{1,0:T(4,128)S(1)} collective-permute-done((f32[4,1024]{1,0:T(4,128)S(1)}, f32[4,1024]{1,0:T(4,128)S(1)}, u32[]{:S(2)}, u32[]{:S(2)}) %collective-permute-start.5) | collective-permute-done | bytes 16416 | tf_op jit(solution)/shard_map/ppermute | solution.py:230
  43.5 2.0 %collective-permute-start.6 = (f32[2,1024]{1,0:T(2,128)S(1)}, f32[2,1024]{1,0:T(2,128)S(1)}, u32[]{:S(2)}, u32[]{:S(2)}) collective-permute-start(f32[2,1024]{1,0:T(2,128)S(1)} %slice.55), channel_id=1, source_target_pairs={{0,1},{1,0},{2,3},{3,2},{4,5},{5,4},{6,7},{7,6},{8,9},{9,8},{10,11... | collective-permute-start | bytes 24584 | tf_op jit(solution)/shard_map/ppermute | solution.py:230
  45.5 1.7 %collective-permute-done.6 = f32[2,1024]{1,0:T(2,128)S(1)} collective-permute-done((f32[2,1024]{1,0:T(2,128)S(1)}, f32[2,1024]{1,0:T(2,128)S(1)}, u32[]{:S(2)}, u32[]{:S(2)}) %collective-permute-start.6) | collective-permute-done | bytes 8224 | tf_op jit(solution)/shard_map/ppermute | solution.py:230
  47.2 0.6 %slice_add_fusion.2 = f32[2,1024]{1,0:T(2,128)} fusion(f32[2,1024]{1,0:T(2,128)S(1)} %collective-permute-done.6, f32[4,1024]{1,0:T(4,128)S(1)} %slice_add_fusion), kind=kLoop, calls=%fused_computation.6 | loop fusion | flops 2048 | bytes 24576 | tf_op jit(solution)/shard_map/add | solution.py:243
  (7 shorter events, 0.1 us)
Async XLA Ops:
  0.0 11.4 %copy-start.1 = (f32[512,2,512]{2,1,0:T(2,128)S(1)}, f32[512,2,512]{2,1,0:T(2,128)}, u32[]{:S(2)}) copy-start(f32[512,2,512]{2,1,0:T(2,128)} %own.1) | copy-start | bytes 6291460
  0.0 11.4 %copy-start = (f32[16,128,512]{2,1,0:T(8,128)S(1)}, f32[16,128,512]{2,1,0:T(8,128)}, u32[]{:S(2)}) copy-start(f32[16,128,512]{2,1,0:T(8,128)} %amp.1) | copy-start | bytes 12582916
  0.0 11.4 %collective-permute-start = (f32[512,2,512]{2,1,0:T(2,128)}, f32[512,2,512]{2,1,0:T(2,128)S(1)}, u32[]{:S(2)}, u32[]{:S(2)}) collective-permute-start(f32[512,2,512]{2,1,0:T(2,128)} %own.1), channel_id=1, source_target_pairs={{0,8},{8,0},{16,24},{24,16},{1,9},{9,1},{17,25},{25,17},{2,10},{10... | collective-permute-start | bytes 6291464 | tf_op jit(solution)/shard_map/ppermute | solution.py:230
  0.5 1.2 %copy-start.2 = (f32[16,4096]{1,0:T(8,128)S(1)}, f32[16,4096]{1,0:T(8,128)}, u32[]{:S(2)}) copy-start(f32[16,4096]{1,0:T(8,128)} %amps_hbm.1) | copy-start | bytes 786436
  8.6 24.8 %collective-permute-start.1 = (f32[2,2,1024]{2,1,0:T(2,128)S(1)}, f32[2,2,1024]{2,1,0:T(2,128)S(1)}, u32[]{:S(2)}, u32[]{:S(2)}) collective-permute-start(f32[2,2,1024]{2,1,0:T(2,128)S(1)} %get-tuple-element.29), channel_id=1, source_target_pairs={{0,16},{8,24},{16,0},{24,8},{1,17},{9,25},{17,1},{25,9},{2,18},{10... | collective-permute-start | bytes 49160 | tf_op jit(solution)/shard_map/ppermute | solution.py:230
  11.4 22.0 %collective-permute-start.2 = (f32[2,2,1024]{2,1,0:T(2,128)S(1)}, f32[2,2,1024]{2,1,0:T(2,128)S(1)}, u32[]{:S(2)}, u32[]{:S(2)}) collective-permute-start(f32[2,2,1024]{2,1,0:T(2,128)S(1)} %get-tuple-element.30), channel_id=1, source_target_pairs={{0,24},{8,16},{16,8},{24,0},{1,25},{9,17},{17,9},{25,1},{2,26},{10... | collective-permute-start | bytes 49160 | tf_op jit(solution)/shard_map/ppermute | solution.py:230
  33.4 1.3 %collective-permute-start.3 = (f32[2,8,1024]{2,1,0:T(8,128)S(1)}, f32[2,8,1024]{2,1,0:T(8,128)S(1)}, u32[]{:S(2)}, u32[]{:S(2)}) collective-permute-start(f32[2,8,1024]{2,1,0:T(8,128)S(1)} %get-tuple-element.32), channel_id=1, source_target_pairs={{0,8},{8,0},{16,24},{24,16},{1,9},{9,1},{17,25},{25,17},{2,10},{10... | collective-permute-start | bytes 196616 | tf_op jit(solution)/shard_map/ppermute | solution.py:230
  34.8 4.0 %collective-permute-start.4 = (f32[8,1024]{1,0:T(8,128)S(1)}, f32[8,1024]{1,0:T(8,128)S(1)}, u32[]{:S(2)}, u32[]{:S(2)}) collective-permute-start(f32[8,1024]{1,0:T(8,128)S(1)} %slice_bitcast_fusion), channel_id=1, source_target_pairs={{0,4},{4,0},{1,5},{5,1},{2,6},{6,2},{3,7},{7,3},{8,12},{12,8},{9,1... | collective-permute-start | bytes 98312 | tf_op jit(solution)/shard_map/ppermute | solution.py:230
  38.8 4.7 %collective-permute-start.5 = (f32[4,1024]{1,0:T(4,128)S(1)}, f32[4,1024]{1,0:T(4,128)S(1)}, u32[]{:S(2)}, u32[]{:S(2)}) collective-permute-start(f32[4,1024]{1,0:T(4,128)S(1)} %slice.53), channel_id=1, source_target_pairs={{0,2},{1,3},{2,0},{3,1},{4,6},{5,7},{6,4},{7,5},{8,10},{9,11},{10,... | collective-permute-start | bytes 49160 | tf_op jit(solution)/shard_map/ppermute | solution.py:230
  43.5 3.7 %collective-permute-start.6 = (f32[2,1024]{1,0:T(2,128)S(1)}, f32[2,1024]{1,0:T(2,128)S(1)}, u32[]{:S(2)}, u32[]{:S(2)}) collective-permute-start(f32[2,1024]{1,0:T(2,128)S(1)} %slice.55), channel_id=1, source_target_pairs={{0,1},{1,0},{2,3},{3,2},{4,5},{5,4},{6,7},{7,6},{8,9},{9,8},{10,11... | collective-permute-start | bytes 24584 | tf_op jit(solution)/shard_map/ppermute | solution.py:230

commit v5 on v4

--- a/solution.py
+++ b/solution.py
@@ -233,15 +233,16 @@
 def fast(grp_count, exc_count, col_count, window_factor, fitted_factor, pair_amps, cycle_amps, panel):
     other = swap(window_factor, "grp", grp_count, 1)
     near, far, across = cycle_slots(cycle_amps, panel)
+    keep, send = ladder_slots(window_factor, other, pair_amps, fitted_factor, near)
+    keep, send, far, across = lax.optimization_barrier((keep, send, far, across))
+    total = keep + swap(send, "grp", grp_count, 1)
     one, two = swap(far, "grp", grp_count, 2), swap(across, "grp", grp_count, 3)
-    keep, send = ladder_slots(window_factor, other, pair_amps, fitted_factor, near)
-    keep, send, one, two = lax.optimization_barrier((keep, send, one, two))
-    total = (keep + swap(send, "grp", grp_count, 1)).at[:, :NI].add(one + two)
-    total = total[0] + swap(total[1], "exc", exc_count, 1)
     bit = col_count // 2
     while bit:
-        total = total[: bit * NI] + swap(total[bit * NI :], "col", col_count, bit)
+        total = total[:, : bit * NI] + swap(total[:, bit * NI :], "col", col_count, bit)
         bit //= 2
+    total = total + (one + two)
+    total = total[0] + swap(total[1], "exc", exc_count, 1)
     return total
 
 

time: 48 us -> 46.3 us (0.965)
  waiting for transfers between devices: 6.63 us -> 4.8 us
    ppermute x7, waiting for transfers between devices: 6.63 us -> 4.8 us  [swap(): return lax.ppermute(x, axis, [(n, n ^ bit) for n in range(size)])]
    add x1, other arithmetic: 0.01 us -> 0.6 us  [fast(): total = total[0] + swap(total[1], 'exc', exc_count, 1)]
    add x3, other arithmetic: 0.62 us -> 0.04 us  [the longest x1 0.02 us: fast(): total = total + (one + two)]
  transfers between devices with their start and end apart: 7 -> 7, of which waited for: 4 -> 5; matrix products, arithmetic and copies ran while one was open for 0% -> 0% of each run, Pallas kernels for 61% -> 15%
where the time goes in v5:
time: 46.3 us; the launch traced here: 46.2 us
  Pallas kernels  29 us (63%)
  starting transfers between devices  10.5 us (23%)
  waiting for transfers between devices  4.8 us (10%)
  local copies, waits for them, and re-layouts  1.2 us (3%)
  other arithmetic  0.64 us (1%)
    pallas_call x1, Pallas kernels, ladder_slots(): pl.pallas_call(ladder_kernel, out_shape=(out, out), in_specs=[pl.BlockSpe...  22 us
    ppermute x7, starting transfers between devices, swap(): return lax.ppermute(x, axis, [(n, n ^ bit) for n in range(size)])  10.5 us
    pallas_call x1, Pallas kernels, cycle_slots(): pl.pallas_call(cycle_kernel, out_shape=(near, far, far), in_specs=[pl.Blo...  6.96 us
    ppermute x7, waiting for transfers between devices, swap(): return lax.ppermute(x, axis, [(n, n ^ bit) for n in range(size)])  4.8 us
    unnamed x6, local copies, waits for them, and re-layouts  1.18 us
  transfers between devices with their start and end apart: 7, of which 5 were waited for; matrix products, arithmetic and copies ran while one was open for 0% of the time, Pallas kernels for 15%

profile of v5, /device:TPU:0, one launch (start us, length us, event | category | flops | bytes accessed | tf_op | source)
XLA Modules:
  0.0 46.2 jit_solution(17136122408593970908)
XLA Ops:
  0.0 0.0 copy-start.1
  0.0 0.0 copy-start
  0.0 0.5 collective-permute-start
  0.5 0.0 copy-start.2
  0.5 1.2 %copy-done.2 = f32[16,4096]{1,0:T(8,128)S(1)} copy-done((f32[16,4096]{1,0:T(8,128)S(1)}, f32[16,4096]{1,0:T(8,128)}, u32[]{:S(2)}) %copy-start.2) | copy-done | bytes 262168
  1.6 7.0 %shard_map.55 = (f32[4,2,1024]{2,1,0:T(2,128)S(1)}, f32[2,2,1024]{2,1,0:T(2,128)S(1)}, f32[2,2,1024]{2,1,0:T(2,128)S(1)}) custom-call(f32[16,4096]{1,0:T(8,128)S(1)} %copy-done.2, f32[4096,1024]{1,0:T(8,128)} %panel_ref.1), custom_call_target="tpu_custom_call" | custom-call | flops 402653184 | bytes 16777216 | tf_op jit(solution)/shard_map/pallas_call | solution.py:87
  8.6 0.0 collective-permute-done.other
  8.6 0.0 copy-done.1
  8.6 0.0 copy-done
  8.6 22.0 %shard_map.56 = (f32[2,8,1024]{2,1,0:T(8,128)S(1)}, f32[2,8,1024]{2,1,0:T(8,128)S(1)}) custom-call(f32[512,2,512]{2,1,0:T(2,128)S(1)} %copy-done.1, f32[512,2,512]{2,1,0:T(2,128)S(1)} %collective-permute-done.other, f32[16,128,512]{2,1,0:T(8,128)S(1)} %copy-done, f32[512,128,512]{2,1,0:T(8,128)} %fitted_hbm.1, f32[4,2,1024]{2,1,0:T(2,128)S(1)} %get-tuple-element.14.near_ref), custom_call_target="tpu_custom_call" | custom-call | flops 12884901888 | bytes 67108864 | tf_op jit(solution)/shard_map/pallas_call | solution.py:201
  30.6 0.4 collective-permute-start.1
  31.0 1.0 %collective-permute-done.1 = f32[2,8,1024]{2,1,0:T(8,128)S(1)} collective-permute-done((f32[2,8,1024]{2,1,0:T(8,128)S(1)}, f32[2,8,1024]{2,1,0:T(8,128)S(1)}, u32[]{:S(2)}, u32[]{:S(2)}) %collective-permute-start.1) | collective-permute-done | bytes 65568 | tf_op jit(solution)/shard_map/ppermute | solution.py:230
  32.0 3.9 %collective-permute-start.2 = (f32[2,4,1024]{2,1,0:T(4,128)S(1)}, f32[2,4,1024]{2,1,0:T(4,128)S(1)}, u32[]{:S(2)}, u32[]{:S(2)}) collective-permute-start(f32[2,4,1024]{2,1,0:T(4,128)S(1)} %slice.25), channel_id=1, source_target_pairs={{0,2},{1,3},{2,0},{3,1},{4,6},{5,7},{6,4},{7,5},{8,10},{9,11},{10,... | collective-permute-start | bytes 98312 | tf_op jit(solution)/shard_map/ppermute | solution.py:230
  35.9 1.5 %collective-permute-start.4 = (f32[2,2,1024]{2,1,0:T(2,128)S(1)}, f32[2,2,1024]{2,1,0:T(2,128)S(1)}, u32[]{:S(2)}, u32[]{:S(2)}) collective-permute-start(f32[2,2,1024]{2,1,0:T(2,128)S(1)} %get-tuple-element.21), channel_id=1, source_target_pairs={{0,16},{8,24},{16,0},{24,8},{1,17},{9,25},{17,1},{25,9},{2,18},{10... | collective-permute-start | bytes 49160 | tf_op jit(solution)/shard_map/ppermute | solution.py:230
  37.4 0.0 collective-permute-start.5
  37.4 0.4 collective-permute-done.2
  37.8 2.0 %collective-permute-start.3 = (f32[2,2,1024]{2,1,0:T(2,128)S(1)}, f32[2,2,1024]{2,1,0:T(2,128)S(1)}, u32[]{:S(2)}, u32[]{:S(2)}) collective-permute-start(f32[2,2,1024]{2,1,0:T(2,128)S(1)} %slice.27), channel_id=1, source_target_pairs={{0,1},{1,0},{2,3},{3,2},{4,5},{5,4},{6,7},{7,6},{8,9},{9,8},{10,11... | collective-permute-start | bytes 49160 | tf_op jit(solution)/shard_map/ppermute | solution.py:230
  39.8 0.0 collective-permute-done.4
  39.8 0.8 %collective-permute-done.5 = f32[2,2,1024]{2,1,0:T(2,128)S(1)} collective-permute-done((f32[2,2,1024]{2,1,0:T(2,128)S(1)}, f32[2,2,1024]{2,1,0:T(2,128)S(1)}, u32[]{:S(2)}, u32[]{:S(2)}) %collective-permute-start.5) | collective-permute-done | bytes 16416 | tf_op jit(solution)/shard_map/ppermute | solution.py:230
  40.6 1.0 %collective-permute-done.3 = f32[2,2,1024]{2,1,0:T(2,128)S(1)} collective-permute-done((f32[2,2,1024]{2,1,0:T(2,128)S(1)}, f32[2,2,1024]{2,1,0:T(2,128)S(1)}, u32[]{:S(2)}, u32[]{:S(2)}) %collective-permute-start.3) | collective-permute-done | bytes 16416 | tf_op jit(solution)/shard_map/ppermute | solution.py:230
  41.6 2.3 %collective-permute-start.6 = (f32[2,1024]{1,0:T(2,128)S(1)}, f32[2,1024]{1,0:T(2,128)S(1)}, u32[]{:S(2)}, u32[]{:S(2)}) collective-permute-start(f32[2,1024]{1,0:T(2,128)S(1)} %slice_bitcast_fusion), channel_id=1, source_target_pairs={{0,4},{4,0},{1,5},{5,1},{2,6},{6,2},{3,7},{7,3},{8,12},{12,8},{9,1... | collective-permute-start | bytes 24584 | tf_op jit(solution)/shard_map/ppermute | solution.py:230
  43.9 1.6 %collective-permute-done.6 = f32[2,1024]{1,0:T(2,128)S(1)} collective-permute-done((f32[2,1024]{1,0:T(2,128)S(1)}, f32[2,1024]{1,0:T(2,128)S(1)}, u32[]{:S(2)}, u32[]{:S(2)}) %collective-permute-start.6) | collective-permute-done | bytes 8224 | tf_op jit(solution)/shard_map/ppermute | solution.py:230
  45.6 0.6 %fusion.1 = f32[2,1024]{1,0:T(2,128)} fusion(f32[2,1024]{1,0:T(2,128)S(1)} %collective-permute-done.6, f32[2,2,1024]{2,1,0:T(2,128)S(1)} %fusion), kind=kLoop, calls=%fused_computation.5 | loop fusion | flops 2048 | bytes 24576 | tf_op jit(solution)/shard_map/add | solution.py:245
  (6 shorter events, 0.1 us)
Async XLA Ops:
  0.0 8.6 %copy-start.1 = (f32[512,2,512]{2,1,0:T(2,128)S(1)}, f32[512,2,512]{2,1,0:T(2,128)}, u32[]{:S(2)}) copy-start(f32[512,2,512]{2,1,0:T(2,128)} %own.1) | copy-start | bytes 6291460
  0.0 8.6 %copy-start = (f32[16,128,512]{2,1,0:T(8,128)S(1)}, f32[16,128,512]{2,1,0:T(8,128)}, u32[]{:S(2)}) copy-start(f32[16,128,512]{2,1,0:T(8,128)} %amp.1) | copy-start | bytes 12582916
  0.0 8.6 %collective-permute-start = (f32[512,2,512]{2,1,0:T(2,128)}, f32[512,2,512]{2,1,0:T(2,128)S(1)}, u32[]{:S(2)}, u32[]{:S(2)}) collective-permute-start(f32[512,2,512]{2,1,0:T(2,128)} %own.1), channel_id=1, source_target_pairs={{0,8},{8,0},{16,24},{24,16},{1,9},{9,1},{17,25},{25,17},{2,10},{10... | collective-permute-start | bytes 6291464 | tf_op jit(solution)/shard_map/ppermute | solution.py:230
  0.5 1.2 %copy-start.2 = (f32[16,4096]{1,0:T(8,128)S(1)}, f32[16,4096]{1,0:T(8,128)}, u32[]{:S(2)}) copy-start(f32[16,4096]{1,0:T(8,128)} %amps_hbm.1) | copy-start | bytes 786436
  30.6 1.3 %collective-permute-start.1 = (f32[2,8,1024]{2,1,0:T(8,128)S(1)}, f32[2,8,1024]{2,1,0:T(8,128)S(1)}, u32[]{:S(2)}, u32[]{:S(2)}) collective-permute-start(f32[2,8,1024]{2,1,0:T(8,128)S(1)} %get-tuple-element.20), channel_id=1, source_target_pairs={{0,8},{8,0},{16,24},{24,16},{1,9},{9,1},{17,25},{25,17},{2,10},{10... | collective-permute-start | bytes 196616 | tf_op jit(solution)/shard_map/ppermute | solution.py:230
  32.0 5.8 %collective-permute-start.2 = (f32[2,4,1024]{2,1,0:T(4,128)S(1)}, f32[2,4,1024]{2,1,0:T(4,128)S(1)}, u32[]{:S(2)}, u32[]{:S(2)}) collective-permute-start(f32[2,4,1024]{2,1,0:T(4,128)S(1)} %slice.25), channel_id=1, source_target_pairs={{0,2},{1,3},{2,0},{3,1},{4,6},{5,7},{6,4},{7,5},{8,10},{9,11},{10,... | collective-permute-start | bytes 98312 | tf_op jit(solution)/shard_map/ppermute | solution.py:230
  35.9 3.9 %collective-permute-start.4 = (f32[2,2,1024]{2,1,0:T(2,128)S(1)}, f32[2,2,1024]{2,1,0:T(2,128)S(1)}, u32[]{:S(2)}, u32[]{:S(2)}) collective-permute-start(f32[2,2,1024]{2,1,0:T(2,128)S(1)} %get-tuple-element.21), channel_id=1, source_target_pairs={{0,16},{8,24},{16,0},{24,8},{1,17},{9,25},{17,1},{25,9},{2,18},{10... | collective-permute-start | bytes 49160 | tf_op jit(solution)/shard_map/ppermute | solution.py:230
  37.4 3.2 %collective-permute-start.5 = (f32[2,2,1024]{2,1,0:T(2,128)S(1)}, f32[2,2,1024]{2,1,0:T(2,128)S(1)}, u32[]{:S(2)}, u32[]{:S(2)}) collective-permute-start(f32[2,2,1024]{2,1,0:T(2,128)S(1)} %get-tuple-element.22), channel_id=1, source_target_pairs={{0,24},{8,16},{16,8},{24,0},{1,25},{9,17},{17,9},{25,1},{2,26},{10... | collective-permute-start | bytes 49160 | tf_op jit(solution)/shard_map/ppermute | solution.py:230
  37.8 3.8 %collective-permute-start.3 = (f32[2,2,1024]{2,1,0:T(2,128)S(1)}, f32[2,2,1024]{2,1,0:T(2,128)S(1)}, u32[]{:S(2)}, u32[]{:S(2)}) collective-permute-start(f32[2,2,1024]{2,1,0:T(2,128)S(1)} %slice.27), channel_id=1, source_target_pairs={{0,1},{1,0},{2,3},{3,2},{4,5},{5,4},{6,7},{7,6},{8,9},{9,8},{10,11... | collective-permute-start | bytes 49160 | tf_op jit(solution)/shard_map/ppermute | solution.py:230
  41.6 3.9 %collective-permute-start.6 = (f32[2,1024]{1,0:T(2,128)S(1)}, f32[2,1024]{1,0:T(2,128)S(1)}, u32[]{:S(2)}, u32[]{:S(2)}) collective-permute-start(f32[2,1024]{1,0:T(2,128)S(1)} %slice_bitcast_fusion), channel_id=1, source_target_pairs={{0,4},{4,0},{1,5},{5,1},{2,6},{6,2},{3,7},{7,3},{8,12},{12,8},{9,1... | collective-permute-start | bytes 24584 | tf_op jit(solution)/shard_map/ppermute | solution.py:230

commit v6 on v5

--- a/solution.py
+++ b/solution.py
@@ -179,9 +179,12 @@
             def _():
                 fetch(step + SLOTS, slot).start()
 
+    order = [0]
+    while len(order) < NJ // 2:
+        order = [2 * n for n in order] + [2 * n + 1 for n in order]
     for target, out in ((0, keep_ref), (1, send_ref)):
         for far in range(2):
-            for away in range(NJ // 2):
+            for place_in, away in enumerate(order):
                 for i in range(NI):
                     for j in range(2):
                         pair = i * NJ + (col ^ away) * 2 + j
@@ -190,7 +193,7 @@
                         value = total[pl.ds(row, 1), :]
                         if away == 0:
                             value += near_ref[target * 2 + far, pl.ds(i, 1), columns]
-                        out[far, pl.ds(away * NI + i, 1), columns] = value
+                        out[far, pl.ds(place_in * NI + i, 1), columns] = value
 
 
 def ladder_slots(own, other, pair_amps, fitted_factor, near):
@@ -237,10 +240,11 @@
     keep, send, far, across = lax.optimization_barrier((keep, send, far, across))
     total = keep + swap(send, "grp", grp_count, 1)
     one, two = swap(far, "grp", grp_count, 2), swap(across, "grp", grp_count, 3)
-    bit = col_count // 2
-    while bit:
-        total = total[:, : bit * NI] + swap(total[:, bit * NI :], "col", col_count, bit)
-        bit //= 2
+    bit = 1
+    while bit < col_count:
+        count = total.shape[1] // 2
+        total = total[:, :count] + swap(total[:, count:], "col", col_count, bit)
+        bit *= 2
     total = total + (one + two)
     total = total[0] + swap(total[1], "exc", exc_count, 1)
     return total

time: 46.3 us -> 46.1 us (level)
  transfers between devices with their start and end apart: 7 -> 7, of which waited for: 5 -> 4; matrix products, arithmetic and copies ran while one was open for 0% -> 0% of each run, Pallas kernels for 15% -> 15%
where the time goes in v6:
time: 46.1 us; the launch traced here: 46 us
  Pallas kernels  29 us (63%)
  starting transfers between devices  10.2 us (22%)
  waiting for transfers between devices  4.83 us (10%)
  local copies, waits for them, and re-layouts  1.2 us (3%)
  other arithmetic  0.64 us (1%)
    pallas_call x1, Pallas kernels, ladder_slots(): pl.pallas_call(ladder_kernel, out_shape=(out, out), in_specs=[pl.BlockSpe...  22 us
    ppermute x7, starting transfers between devices, swap(): return lax.ppermute(x, axis, [(n, n ^ bit) for n in range(size)])  10.2 us
    pallas_call x1, Pallas kernels, cycle_slots(): pl.pallas_call(cycle_kernel, out_shape=(near, far, far), in_specs=[pl.Blo...  6.96 us
    ppermute x7, waiting for transfers between devices, swap(): return lax.ppermute(x, axis, [(n, n ^ bit) for n in range(size)])  4.83 us
    unnamed x6, local copies, waits for them, and re-layouts  1.18 us
  transfers between devices with their start and end apart: 7, of which 4 were waited for; matrix products, arithmetic and copies ran while one was open for 0% of the time, Pallas kernels for 15%

profile of v6, /device:TPU:0, one launch (start us, length us, event | category | flops | bytes accessed | tf_op | source)
XLA Modules:
  0.0 46.0 jit_solution(15243806813955522702)
XLA Ops:
  0.0 0.0 copy-start.1
  0.0 0.0 copy-start
  0.0 0.5 collective-permute-start
  0.5 0.0 copy-start.2
  0.5 1.2 %copy-done.2 = f32[16,4096]{1,0:T(8,128)S(1)} copy-done((f32[16,4096]{1,0:T(8,128)S(1)}, f32[16,4096]{1,0:T(8,128)}, u32[]{:S(2)}) %copy-start.2) | copy-done | bytes 262168
  1.6 7.0 %shard_map.55 = (f32[4,2,1024]{2,1,0:T(2,128)S(1)}, f32[2,2,1024]{2,1,0:T(2,128)S(1)}, f32[2,2,1024]{2,1,0:T(2,128)S(1)}) custom-call(f32[16,4096]{1,0:T(8,128)S(1)} %copy-done.2, f32[4096,1024]{1,0:T(8,128)} %panel_ref.1), custom_call_target="tpu_custom_call" | custom-call | flops 402653184 | bytes 16777216 | tf_op jit(solution)/shard_map/pallas_call | solution.py:87
  8.6 0.0 collective-permute-done.other
  8.6 0.0 copy-done.1
  8.6 0.0 copy-done
  8.6 22.0 %shard_map.56 = (f32[2,8,1024]{2,1,0:T(8,128)S(1)}, f32[2,8,1024]{2,1,0:T(8,128)S(1)}) custom-call(f32[512,2,512]{2,1,0:T(2,128)S(1)} %copy-done.1, f32[512,2,512]{2,1,0:T(2,128)S(1)} %collective-permute-done.other, f32[16,128,512]{2,1,0:T(8,128)S(1)} %copy-done, f32[512,128,512]{2,1,0:T(8,128)} %fitted_hbm.1, f32[4,2,1024]{2,1,0:T(2,128)S(1)} %get-tuple-element.14.near_ref), custom_call_target="tpu_custom_call" | custom-call | flops 12884901888 | bytes 67108864 | tf_op jit(solution)/shard_map/pallas_call | solution.py:204
  30.6 0.4 collective-permute-start.1
  31.0 1.0 %collective-permute-done.1 = f32[2,8,1024]{2,1,0:T(8,128)S(1)} collective-permute-done((f32[2,8,1024]{2,1,0:T(8,128)S(1)}, f32[2,8,1024]{2,1,0:T(8,128)S(1)}, u32[]{:S(2)}, u32[]{:S(2)}) %collective-permute-start.1) | collective-permute-done | bytes 65568 | tf_op jit(solution)/shard_map/ppermute | solution.py:233
  32.0 2.9 %collective-permute-start.2 = (f32[2,4,1024]{2,1,0:T(4,128)S(1)}, f32[2,4,1024]{2,1,0:T(4,128)S(1)}, u32[]{:S(2)}, u32[]{:S(2)}) collective-permute-start(f32[2,4,1024]{2,1,0:T(4,128)S(1)} %slice.25), channel_id=1, source_target_pairs={{0,1},{1,0},{2,3},{3,2},{4,5},{5,4},{6,7},{7,6},{8,9},{9,8},{10,11... | collective-permute-start | bytes 98312 | tf_op jit(solution)/shard_map/ppermute | solution.py:233
  34.8 1.5 %collective-permute-start.4 = (f32[2,2,1024]{2,1,0:T(2,128)S(1)}, f32[2,2,1024]{2,1,0:T(2,128)S(1)}, u32[]{:S(2)}, u32[]{:S(2)}) collective-permute-start(f32[2,2,1024]{2,1,0:T(2,128)S(1)} %get-tuple-element.21), channel_id=1, source_target_pairs={{0,16},{8,24},{16,0},{24,8},{1,17},{9,25},{17,1},{25,9},{2,18},{10... | collective-permute-start | bytes 49160 | tf_op jit(solution)/shard_map/ppermute | solution.py:233
  36.4 0.0 collective-permute-start.5
  36.4 0.4 collective-permute-done.2
  36.8 3.1 %collective-permute-start.3 = (f32[2,2,1024]{2,1,0:T(2,128)S(1)}, f32[2,2,1024]{2,1,0:T(2,128)S(1)}, u32[]{:S(2)}, u32[]{:S(2)}) collective-permute-start(f32[2,2,1024]{2,1,0:T(2,128)S(1)} %slice.27), channel_id=1, source_target_pairs={{0,2},{1,3},{2,0},{3,1},{4,6},{5,7},{6,4},{7,5},{8,10},{9,11},{10,... | collective-permute-start | bytes 49160 | tf_op jit(solution)/shard_map/ppermute | solution.py:233
  39.9 0.0 collective-permute-done.4
  39.9 0.0 collective-permute-done.5
  39.9 1.7 %collective-permute-done.3 = f32[2,2,1024]{2,1,0:T(2,128)S(1)} collective-permute-done((f32[2,2,1024]{2,1,0:T(2,128)S(1)}, f32[2,2,1024]{2,1,0:T(2,128)S(1)}, u32[]{:S(2)}, u32[]{:S(2)}) %collective-permute-start.3) | collective-permute-done | bytes 16416 | tf_op jit(solution)/shard_map/ppermute | solution.py:233
  41.6 1.9 %collective-permute-start.6 = (f32[2,1024]{1,0:T(2,128)S(1)}, f32[2,1024]{1,0:T(2,128)S(1)}, u32[]{:S(2)}, u32[]{:S(2)}) collective-permute-start(f32[2,1024]{1,0:T(2,128)S(1)} %slice_bitcast_fusion), channel_id=1, source_target_pairs={{0,4},{4,0},{1,5},{5,1},{2,6},{6,2},{3,7},{7,3},{8,12},{12,8},{9,1... | collective-permute-start | bytes 24584 | tf_op jit(solution)/shard_map/ppermute | solution.py:233
  43.6 1.8 %collective-permute-done.6 = f32[2,1024]{1,0:T(2,128)S(1)} collective-permute-done((f32[2,1024]{1,0:T(2,128)S(1)}, f32[2,1024]{1,0:T(2,128)S(1)}, u32[]{:S(2)}, u32[]{:S(2)}) %collective-permute-start.6) | collective-permute-done | bytes 8224 | tf_op jit(solution)/shard_map/ppermute | solution.py:233
  45.4 0.6 %fusion.1 = f32[2,1024]{1,0:T(2,128)} fusion(f32[2,1024]{1,0:T(2,128)S(1)} %collective-permute-done.6, f32[2,2,1024]{2,1,0:T(2,128)S(1)} %fusion), kind=kLoop, calls=%fused_computation.5 | loop fusion | flops 2048 | bytes 24576 | tf_op jit(solution)/shard_map/add | solution.py:249
  (6 shorter events, 0.1 us)
Async XLA Ops:
  0.0 8.6 %copy-start.1 = (f32[512,2,512]{2,1,0:T(2,128)S(1)}, f32[512,2,512]{2,1,0:T(2,128)}, u32[]{:S(2)}) copy-start(f32[512,2,512]{2,1,0:T(2,128)} %own.1) | copy-start | bytes 6291460
  0.0 8.6 %copy-start = (f32[16,128,512]{2,1,0:T(8,128)S(1)}, f32[16,128,512]{2,1,0:T(8,128)}, u32[]{:S(2)}) copy-start(f32[16,128,512]{2,1,0:T(8,128)} %amp.1) | copy-start | bytes 12582916
  0.0 8.6 %collective-permute-start = (f32[512,2,512]{2,1,0:T(2,128)}, f32[512,2,512]{2,1,0:T(2,128)S(1)}, u32[]{:S(2)}, u32[]{:S(2)}) collective-permute-start(f32[512,2,512]{2,1,0:T(2,128)} %own.1), channel_id=1, source_target_pairs={{0,8},{8,0},{16,24},{24,16},{1,9},{9,1},{17,25},{25,17},{2,10},{10... | collective-permute-start | bytes 6291464 | tf_op jit(solution)/shard_map/ppermute | solution.py:233
  0.5 1.2 %copy-start.2 = (f32[16,4096]{1,0:T(8,128)S(1)}, f32[16,4096]{1,0:T(8,128)}, u32[]{:S(2)}) copy-start(f32[16,4096]{1,0:T(8,128)} %amps_hbm.1) | copy-start | bytes 786436
  30.6 1.3 %collective-permute-start.1 = (f32[2,8,1024]{2,1,0:T(8,128)S(1)}, f32[2,8,1024]{2,1,0:T(8,128)S(1)}, u32[]{:S(2)}, u32[]{:S(2)}) collective-permute-start(f32[2,8,1024]{2,1,0:T(8,128)S(1)} %get-tuple-element.20), channel_id=1, source_target_pairs={{0,8},{8,0},{16,24},{24,16},{1,9},{9,1},{17,25},{25,17},{2,10},{10... | collective-permute-start | bytes 196616 | tf_op jit(solution)/shard_map/ppermute | solution.py:233
  32.0 4.8 %collective-permute-start.2 = (f32[2,4,1024]{2,1,0:T(4,128)S(1)}, f32[2,4,1024]{2,1,0:T(4,128)S(1)}, u32[]{:S(2)}, u32[]{:S(2)}) collective-permute-start(f32[2,4,1024]{2,1,0:T(4,128)S(1)} %slice.25), channel_id=1, source_target_pairs={{0,1},{1,0},{2,3},{3,2},{4,5},{5,4},{6,7},{7,6},{8,9},{9,8},{10,11... | collective-permute-start | bytes 98312 | tf_op jit(solution)/shard_map/ppermute | solution.py:233
  34.8 5.0 %collective-permute-start.4 = (f32[2,2,1024]{2,1,0:T(2,128)S(1)}, f32[2,2,1024]{2,1,0:T(2,128)S(1)}, u32[]{:S(2)}, u32[]{:S(2)}) collective-permute-start(f32[2,2,1024]{2,1,0:T(2,128)S(1)} %get-tuple-element.21), channel_id=1, source_target_pairs={{0,16},{8,24},{16,0},{24,8},{1,17},{9,25},{17,1},{25,9},{2,18},{10... | collective-permute-start | bytes 49160 | tf_op jit(solution)/shard_map/ppermute | solution.py:233
  36.4 3.5 %collective-permute-start.5 = (f32[2,2,1024]{2,1,0:T(2,128)S(1)}, f32[2,2,1024]{2,1,0:T(2,128)S(1)}, u32[]{:S(2)}, u32[]{:S(2)}) collective-permute-start(f32[2,2,1024]{2,1,0:T(2,128)S(1)} %get-tuple-element.22), channel_id=1, source_target_pairs={{0,24},{8,16},{16,8},{24,0},{1,25},{9,17},{17,9},{25,1},{2,26},{10... | collective-permute-start | bytes 49160 | tf_op jit(solution)/shard_map/ppermute | solution.py:233
  36.8 4.8 %collective-permute-start.3 = (f32[2,2,1024]{2,1,0:T(2,128)S(1)}, f32[2,2,1024]{2,1,0:T(2,128)S(1)}, u32[]{:S(2)}, u32[]{:S(2)}) collective-permute-start(f32[2,2,1024]{2,1,0:T(2,128)S(1)} %slice.27), channel_id=1, source_target_pairs={{0,2},{1,3},{2,0},{3,1},{4,6},{5,7},{6,4},{7,5},{8,10},{9,11},{10,... | collective-permute-start | bytes 49160 | tf_op jit(solution)/shard_map/ppermute | solution.py:233
  41.6 3.7 %collective-permute-start.6 = (f32[2,1024]{1,0:T(2,128)S(1)}, f32[2,1024]{1,0:T(2,128)S(1)}, u32[]{:S(2)}, u32[]{:S(2)}) collective-permute-start(f32[2,1024]{1,0:T(2,128)S(1)} %slice_bitcast_fusion), channel_id=1, source_target_pairs={{0,4},{4,0},{1,5},{5,1},{2,6},{6,2},{3,7},{7,3},{8,12},{12,8},{9,1... | collective-permute-start | bytes 24584 | tf_op jit(solution)/shard_map/ppermute | solution.py:233
